TPU v7x, 32 devices: a whole 2x2x4 slice. The times are simulated.
32 devices in a mesh: section: 2 (over core), dp: 16 (over z, y, x).
Axes of the slice: x: 2, y: 2, z: 4, core: 2. Of those that a mesh axis runs over, the one named last changes fastest.
Arguments:
- tokens: bfloat16 [2, 8192, 768], P(None, 'dp'), may hold values from -6 to 6
- lengths: int32 [2, 16, 4], P(None, 'dp'), may hold values from 1 to 320, 512 in all within a row
- cotangent: bfloat16 [2, 8192, 768], P(None, 'dp'), may hold values from -6 to 6
- qkv_weight: bfloat16 [2, 768, 2304], P('section', 'dp'), may hold values from -0.21875 to 0.21875
- out_weight: bfloat16 [2, 768, 768], P('section', 'dp'), may hold values from -0.875 to 0.875
- up_weight: bfloat16 [2, 768, 3072], P('section', 'dp'), may hold values from -0.21875 to 0.21875
- down_weight: bfloat16 [2, 3072, 768], P('section', 'dp'), may hold values from -0.109375 to 0.109375
- qkv_bias: bfloat16 [2, 2304], P('section', 'dp'), may hold values from -1.5 to 1.5
- out_bias: bfloat16 [2, 768], P('section', 'dp'), may hold values from -1.5 to 1.5
- up_bias: bfloat16 [2, 3072], P('section', 'dp'), may hold values from -1.5 to 1.5
- down_bias: bfloat16 [2, 768], P('section', 'dp'), may hold values from -1.5 to 1.5
- attn_gain: bfloat16 [2, 768], P('section', 'dp'), may hold values from 0.5 to 1.5
- attn_shift: bfloat16 [2, 768], P('section', 'dp'), may hold values from -1.5 to 1.5
- mlp_gain: bfloat16 [2, 768], P('section', 'dp'), may hold values from 0.5 to 1.5
- mlp_shift: bfloat16 [2, 768], P('section', 'dp'), may hold values from -1.5 to 1.5
Outputs:
- layer_outputs: bfloat16 [2, 2, 8192, 768], P('section', None, 'dp')
- input_grads: float32 [2, 2, 8192, 768], P('section', None, 'dp')
- grad_qkv_weight: float32 [2, 768, 2304], P('section', 'dp')
- grad_out_weight: float32 [2, 768, 768], P('section', 'dp')
- grad_up_weight: float32 [2, 768, 3072], P('section', 'dp')
- grad_down_weight: float32 [2, 3072, 768], P('section', 'dp')
- grad_qkv_bias: float32 [2, 2304], P('section', 'dp')
- grad_out_bias: float32 [2, 768], P('section', 'dp')
- grad_up_bias: float32 [2, 3072], P('section', 'dp')
- grad_down_bias: float32 [2, 768], P('section', 'dp')
- grad_attn_gain: float32 [2, 768], P('section', 'dp')
- grad_attn_shift: float32 [2, 768], P('section', 'dp')
- grad_mlp_gain: float32 [2, 768], P('section', 'dp')
- grad_mlp_shift: float32 [2, 768], P('section', 'dp')
Inputs may be any that keep to these rules, and one draw needn't show every extreme that they name: Each row lengths[m, j, :] sums to 512, and its longest sequence has exactly 320 tokens.
All inputs are finite; a program needn't handle non-finite values.
Results may differ from a plain program's by a relative error of at most 0.012.
Values may be sent and summed in bfloat16 or wider, within the bound.
A program may use at most 256 MiB of HBM per device.

v0:
```python
import jax
import jax.numpy as jnp
from jax import lax
from jax.sharding import PartitionSpec as P

EPSILON = 1e-05
HEAD_WIDTH = 64


def from_behind(value, axis, steps):
    count = lax.axis_size(axis)
    first, last = (max(0, -steps), min(count, count - steps))
    return lax.ppermute(value, axis, [(source, source + steps) for source in range(first, last)])


def layer_norm(values, gain, offset):
    centre = jnp.mean(values, axis=-1, keepdims=True)
    centred = values - centre
    spread = jnp.mean(centred * centred, axis=-1, keepdims=True)
    return centred * lax.rsqrt(spread + EPSILON) * gain + offset


def segment_info(seq_lengths, count):
    ends = jnp.cumsum(seq_lengths)
    starts = ends - seq_lengths
    places = jnp.arange(count, dtype=jnp.int32)
    inside = ((places[:, None] >= starts[None, :]) & (places[:, None] < ends[None, :])).astype(
        jnp.int32
    )
    seq_ids = jnp.sum(inside * jnp.arange(seq_lengths.shape[0], dtype=jnp.int32)[None, :], axis=1)
    positions = places - jnp.sum(inside * starts[None, :], axis=1)
    return (seq_ids, positions)


def angle_tables(positions):
    freqs = 10000.0 ** (-jnp.arange(8, dtype=jnp.float32) / 8.0)
    angles = positions.astype(jnp.float32)[:, None] * freqs[None, :]
    return (jnp.cos(angles)[:, None, :], jnp.sin(angles)[:, None, :])


def rotate(part, cosine, sine):
    first = part[..., :8]
    second = part[..., 8:16]
    return jnp.concatenate(
        [first * cosine - second * sine, second * cosine + first * sine, part[..., 16:]], axis=-1
    )


def unrotate(grad, cosine, sine):
    first = grad[..., :8]
    second = grad[..., 8:16]
    return jnp.concatenate(
        [first * cosine + second * sine, second * cosine - first * sine, grad[..., 16:]], axis=-1
    )


def layer_forward(entry, seq_lengths, gathered):
    qkv_w, out_w, up_w, down_w, qkv_b, out_b, up_b, down_b, gain_a, shift_a, gain_m, shift_m = (
        gathered
    )
    count, width = entry.shape
    heads = width // HEAD_WIDTH
    seq_ids, positions = segment_info(seq_lengths, count)
    normed_a = layer_norm(entry, gain_a.astype(jnp.float32), shift_a.astype(jnp.float32)).astype(
        jnp.bfloat16
    )
    normed_m = layer_norm(entry, gain_m.astype(jnp.float32), shift_m.astype(jnp.float32)).astype(
        jnp.bfloat16
    )
    qkv = jnp.dot(normed_a, qkv_w, preferred_element_type=jnp.float32) + qkv_b.astype(jnp.float32)
    cosine, sine = angle_tables(positions)
    queries = rotate(qkv[:, :width].reshape(count, heads, HEAD_WIDTH), cosine, sine).astype(
        jnp.bfloat16
    )
    keys = rotate(qkv[:, width : 2 * width].reshape(count, heads, HEAD_WIDTH), cosine, sine).astype(
        jnp.bfloat16
    )
    values = qkv[:, 2 * width :].reshape(count, heads, HEAD_WIDTH).astype(jnp.bfloat16)
    allowed = (seq_ids[:, None] == seq_ids[None, :]) & (positions[:, None] >= positions[None, :])
    scores = jnp.einsum("thd,shd->hts", queries, keys, preferred_element_type=jnp.float32) * 0.125
    scores = jnp.where(allowed[None], scores, -1e30)
    top = jnp.max(scores, axis=-1, keepdims=True)
    expo = jnp.exp(scores - top)
    total = jnp.sum(expo, axis=-1, keepdims=True)
    log_total = top + jnp.log(total)
    weights = (expo / total).astype(jnp.bfloat16)
    attended = jnp.einsum("hts,shd->thd", weights, values, preferred_element_type=jnp.float32)
    attended = attended.reshape(count, width).astype(jnp.bfloat16)
    hidden = jnp.dot(normed_m, up_w, preferred_element_type=jnp.float32) + up_b.astype(jnp.float32)
    activated = jax.nn.gelu(hidden, approximate=False).astype(jnp.bfloat16)
    branch_a = jnp.dot(attended, out_w, preferred_element_type=jnp.float32) + out_b.astype(
        jnp.float32
    )
    branch_m = jnp.dot(activated, down_w, preferred_element_type=jnp.float32) + down_b.astype(
        jnp.float32
    )
    result = entry + branch_a + branch_m
    kept = (
        normed_a,
        normed_m,
        queries,
        keys,
        values,
        log_total,
        attended,
        hidden,
        activated,
        allowed,
        cosine,
        sine,
    )
    return (result, kept)


def layer_backward(upstream, entry, kept, gathered):
    qkv_w, out_w, up_w, down_w, qkv_b, out_b, up_b, down_b, gain_a, shift_a, gain_m, shift_m = (
        gathered
    )
    (
        normed_a,
        normed_m,
        queries,
        keys,
        values,
        log_total,
        attended,
        hidden,
        activated,
        allowed,
        cosine,
        sine,
    ) = kept
    count, width = entry.shape
    heads = width // HEAD_WIDTH
    up_low = upstream.astype(jnp.bfloat16)
    grad_down_w = jnp.einsum("tf,td->fd", activated, up_low, preferred_element_type=jnp.float32)
    grad_out_w = jnp.einsum("te,td->ed", attended, up_low, preferred_element_type=jnp.float32)
    grad_rows = jnp.sum(upstream, axis=0)
    d_activated = jnp.einsum("td,fd->tf", up_low, down_w, preferred_element_type=jnp.float32)
    _, gelu_back = jax.vjp(lambda inner: jax.nn.gelu(inner, approximate=False), hidden)
    d_hidden = gelu_back(d_activated)[0].astype(jnp.bfloat16)
    grad_up_w = jnp.einsum("td,tf->df", normed_m, d_hidden, preferred_element_type=jnp.float32)
    grad_up_b = jnp.sum(d_hidden.astype(jnp.float32), axis=0)
    d_normed_m = jnp.einsum("tf,df->td", d_hidden, up_w, preferred_element_type=jnp.float32)
    d_attended = jnp.einsum("te,de->td", up_low, out_w, preferred_element_type=jnp.float32)
    d_attended = d_attended.astype(jnp.bfloat16).reshape(count, heads, HEAD_WIDTH)
    scores = jnp.einsum("thd,shd->hts", queries, keys, preferred_element_type=jnp.float32) * 0.125
    scores = jnp.where(allowed[None], scores, -1e30)
    probs = jnp.exp(scores - log_total)
    d_probs = jnp.einsum("thd,shd->hts", d_attended, values, preferred_element_type=jnp.float32)
    d_values = jnp.einsum(
        "hts,thd->shd", probs.astype(jnp.bfloat16), d_attended, preferred_element_type=jnp.float32
    )
    d_scores = probs * (d_probs - jnp.sum(d_probs * probs, axis=-1, keepdims=True))
    d_scores = d_scores.astype(jnp.bfloat16)
    d_queries = (
        jnp.einsum("hts,shd->thd", d_scores, keys, preferred_element_type=jnp.float32) * 0.125
    )
    d_keys = (
        jnp.einsum("hts,thd->shd", d_scores, queries, preferred_element_type=jnp.float32) * 0.125
    )
    d_qkv = jnp.concatenate(
        [
            unrotate(d_queries, cosine, sine).reshape(count, width),
            unrotate(d_keys, cosine, sine).reshape(count, width),
            d_values.reshape(count, width),
        ],
        axis=1,
    ).astype(jnp.bfloat16)
    grad_qkv_w = jnp.einsum("td,te->de", normed_a, d_qkv, preferred_element_type=jnp.float32)
    grad_qkv_b = jnp.sum(d_qkv.astype(jnp.float32), axis=0)
    d_normed_a = jnp.einsum("te,de->td", d_qkv, qkv_w, preferred_element_type=jnp.float32)
    _, norm_back_a = jax.vjp(
        layer_norm, entry, gain_a.astype(jnp.float32), shift_a.astype(jnp.float32)
    )
    d_entry_a, grad_gain_a, grad_shift_a = norm_back_a(d_normed_a)
    _, norm_back_m = jax.vjp(
        layer_norm, entry, gain_m.astype(jnp.float32), shift_m.astype(jnp.float32)
    )
    d_entry_m, grad_gain_m, grad_shift_m = norm_back_m(d_normed_m)
    d_entry = upstream + d_entry_a + d_entry_m
    grads = (
        grad_qkv_w,
        grad_out_w,
        grad_up_w,
        grad_down_w,
        grad_qkv_b,
        grad_rows,
        grad_up_b,
        grad_rows,
        grad_gain_a,
        grad_shift_a,
        grad_gain_m,
        grad_shift_m,
    )
    return (d_entry, grads)


def on_device(
    tokens,
    lengths,
    cotangent,
    qkv_weight,
    out_weight,
    up_weight,
    down_weight,
    qkv_bias,
    out_bias,
    up_bias,
    down_bias,
    attn_gain,
    attn_shift,
    mlp_gain,
    mlp_shift,
):
    section_index = lax.axis_index("section")
    batches = tokens.shape[0]
    gathered = (
        lax.all_gather(qkv_weight[0], "dp", axis=0, tiled=True),
        lax.all_gather(out_weight[0], "dp", axis=0, tiled=True),
        lax.all_gather(up_weight[0], "dp", axis=0, tiled=True),
        lax.all_gather(down_weight[0], "dp", axis=0, tiled=True),
        lax.all_gather(qkv_bias[0], "dp", axis=0, tiled=True),
        lax.all_gather(out_bias[0], "dp", axis=0, tiled=True),
        lax.all_gather(up_bias[0], "dp", axis=0, tiled=True),
        lax.all_gather(down_bias[0], "dp", axis=0, tiled=True),
        lax.all_gather(attn_gain[0], "dp", axis=0, tiled=True),
        lax.all_gather(attn_shift[0], "dp", axis=0, tiled=True),
        lax.all_gather(mlp_gain[0], "dp", axis=0, tiled=True),
        lax.all_gather(mlp_shift[0], "dp", axis=0, tiled=True),
    )
    received = jnp.zeros(tokens.shape[1:], jnp.bfloat16)
    entries, keeps, results = ([], [], [])
    for moment in range(batches + 1):
        batch_index = jnp.clip(moment - section_index, 0, batches - 1)
        own_tokens = lax.dynamic_index_in_dim(tokens, batch_index, 0, keepdims=False)
        entry = jnp.where(section_index == 0, own_tokens, received).astype(jnp.float32)
        seq_lengths = lax.dynamic_index_in_dim(lengths, batch_index, 0, keepdims=False)[0]
        result, kept = layer_forward(entry, seq_lengths, gathered)
        rounded = result.astype(jnp.bfloat16)
        entries.append(entry)
        keeps.append(kept)
        results.append(rounded)
        if moment < batches:
            received = from_behind(rounded, "section", 1)
    layer_outputs = jnp.stack(
        [
            jnp.where(section_index == 0, results[batch], results[batch + 1])
            for batch in range(batches)
        ]
    )
    gathered = (
        lax.all_gather(qkv_weight[0], "dp", axis=0, tiled=True),
        lax.all_gather(out_weight[0], "dp", axis=0, tiled=True),
        lax.all_gather(up_weight[0], "dp", axis=0, tiled=True),
        lax.all_gather(down_weight[0], "dp", axis=0, tiled=True),
        lax.all_gather(qkv_bias[0], "dp", axis=0, tiled=True),
        lax.all_gather(out_bias[0], "dp", axis=0, tiled=True),
        lax.all_gather(up_bias[0], "dp", axis=0, tiled=True),
        lax.all_gather(down_bias[0], "dp", axis=0, tiled=True),
        lax.all_gather(attn_gain[0], "dp", axis=0, tiled=True),
        lax.all_gather(attn_shift[0], "dp", axis=0, tiled=True),
        lax.all_gather(mlp_gain[0], "dp", axis=0, tiled=True),
        lax.all_gather(mlp_shift[0], "dp", axis=0, tiled=True),
    )
    arriving = jnp.zeros(tokens.shape[1:], jnp.float32)
    totals = None
    backs = []
    for moment in range(batches + 1):
        forward_moment = batches - moment
        batch_number = forward_moment - section_index
        batch_index = jnp.clip(batch_number, 0, batches - 1)
        live_flag = ((batch_number >= 0) & (batch_number < batches)).astype(jnp.float32)
        own_grad = lax.dynamic_index_in_dim(cotangent, batch_index, 0, keepdims=False).astype(
            jnp.float32
        )
        upstream = jnp.where(section_index == 1, own_grad, arriving) * live_flag
        d_entry, grads = layer_backward(
            upstream, entries[forward_moment], keeps[forward_moment], gathered
        )
        totals = grads if totals is None else jax.tree.map(jnp.add, totals, grads)
        backs.append(d_entry)
        if moment < batches:
            arriving = from_behind(d_entry.astype(jnp.bfloat16), "section", -1).astype(jnp.float32)
    input_grads = jnp.stack(
        [
            jnp.where(section_index == 0, backs[batches - batch], backs[batches - 1 - batch])
            for batch in range(batches)
        ]
    )
    reduced = (
        lax.psum_scatter(totals[0], "dp", scatter_dimension=0, tiled=True),
        lax.psum_scatter(totals[1], "dp", scatter_dimension=0, tiled=True),
        lax.psum_scatter(totals[2], "dp", scatter_dimension=0, tiled=True),
        lax.psum_scatter(totals[3], "dp", scatter_dimension=0, tiled=True),
        lax.psum_scatter(totals[4], "dp", scatter_dimension=0, tiled=True),
        lax.psum_scatter(totals[5], "dp", scatter_dimension=0, tiled=True),
        lax.psum_scatter(totals[6], "dp", scatter_dimension=0, tiled=True),
        lax.psum_scatter(totals[7], "dp", scatter_dimension=0, tiled=True),
        lax.psum_scatter(totals[8], "dp", scatter_dimension=0, tiled=True),
        lax.psum_scatter(totals[9], "dp", scatter_dimension=0, tiled=True),
        lax.psum_scatter(totals[10], "dp", scatter_dimension=0, tiled=True),
        lax.psum_scatter(totals[11], "dp", scatter_dimension=0, tiled=True),
    )
    return (layer_outputs[None], input_grads[None]) + tuple((piece[None] for piece in reduced))


def solution(mesh):
    placed = (
        P(None, "dp", None),
        P(None, "dp", None),
        P(None, "dp", None),
        P("section", "dp", None),
        P("section", "dp", None),
        P("section", "dp", None),
        P("section", "dp", None),
        P("section", "dp"),
        P("section", "dp"),
        P("section", "dp"),
        P("section", "dp"),
        P("section", "dp"),
        P("section", "dp"),
        P("section", "dp"),
        P("section", "dp"),
    )
    return jax.shard_map(
        on_device,
        mesh=mesh,
        in_specs=placed,
        out_specs=(
            P("section", None, "dp", None),
            P("section", None, "dp", None),
            P("section", "dp", None),
            P("section", "dp", None),
            P("section", "dp", None),
            P("section", "dp", None),
            P("section", "dp"),
            P("section", "dp"),
            P("section", "dp"),
            P("section", "dp"),
            P("section", "dp"),
            P("section", "dp"),
            P("section", "dp"),
            P("section", "dp"),
        ),
        check_vma=False,
    )
```

profile of v0, /device:TPU:0, one launch (start us, length us, event | category | flops | bytes accessed | tf_op | source)
XLA Modules:
  0.0 1206.2 jit_solution(15022275769976796536)
XLA Ops:
  20.3 79.1 %all-reduce.16 = (bf16[768]{0:T(1024)(128)(2,1)S(1)}, bf16[768]{0:T(1024)(128)(2,1)S(1)}, bf16[3072]{0:T(1024)(128)(2,1)S(1)}, bf16[2304]{0:T(1024)(128)(2,1)S(1...) all-reduce(bf16[768]{0:T(1024)(128)(2,1)S(1)} %dynamic-update-slice, ...), channel_id=9, replica_groups=mesh['section'=2,'dp'=16] {'dp'}, use_global_device_ids=true, to_apply=%add.5 | all-reduce | flops 9984 | bytes 39936
  109.2 4.2 convolution_add_fusion.2
  127.9 3.3 fusion.60
  135.8 3.6 fusion.159
  139.4 28.5 %all-gather.21.cloned.1.call-done = bf16[1,768,3072]{2,1,0:T(8,128)(2,1)} async-done(((bf16[1,48,3072]{2,1,0:T(8,128)(2,1)}), bf16[1,768,3072]{2,1,0:T(8,128)(2,1)}) %all-gather.21.cloned.1.call-update) | async-done | bytes 4718608 | tf_op jit(solution)/shard_map/all_gather | solution.py:221
  167.9 20.0 %multiply_convert_fusion.5 = (bf16[512,3072]{1,0:T(8,128)(2,1)}, f32[512,3072]{1,0:T(8,128)}, f32[512,3072]{1,0:T(8,128)}) fusion(f32[3072]{0:T(1024)S(1)} %copy-done.130, bf16[1,768,3072]{2,1,0:T(8,128)(2,1)} %all-gather.21.cloned.1.call-done, f32[768]{0:T(1024)S(1)} %convert_element_type.375, f32[768]{0:T(1024)S(1)} %convert_element_type.374, ...), kind=kOutput, calls=%fused_computation.71 | convolution fusion | flops 2522480640 | bytes 21258244 | tf_op jit(solution)/shard_map/dot_general | solution.py:89
  187.9 61.9 %all-gather.23.cloned.1.call-done = bf16[1,3072,768]{2,1,0:T(8,128)(2,1)} async-done(((bf16[1,192,768]{2,1,0:T(8,128)(2,1)}), bf16[1,3072,768]{2,1,0:T(8,128)(2,1)}) %all-gather.23.cloned.1.call-update) | async-done | bytes 4718608 | tf_op jit(solution)/shard_map/all_gather | solution.py:222
  249.8 7.0 fusion.46
  256.8 50.4 %all-gather.19.cloned.1.call-done = bf16[1,768,768]{2,1,0:T(8,128)(2,1)} async-done(((bf16[1,48,768]{2,1,0:T(8,128)(2,1)}), bf16[1,768,768]{2,1,0:T(8,128)(2,1)}) %all-gather.19.cloned.1.call-update) | async-done | bytes 1179664 | tf_op jit(solution)/shard_map/all_gather | solution.py:220
  320.7 3.4 copy.125
  332.2 3.3 fusion.61
  340.1 3.7 fusion.158
  343.9 19.8 %multiply_convert_fusion.4 = (bf16[512,3072]{1,0:T(8,128)(2,1)S(1)}, f32[512,3072]{1,0:T(8,128)}, f32[512,3072]{1,0:T(8,128)}) fusion(f32[3072]{0:T(1024)S(1)} %copy-done.131, bf16[1,768,3072]{2,1,0:T(8,128)(2,1)} %all-gather.21.cloned.1.call-done, bf16[512,768]{1,0:T(8,128)(2,1)S(1)} %get-tuple-element.78, f32[768]{0:T(1024)S(1)} %convert_element_type.375, ...), kind=kOutput, calls=%fused_computation.58 | convolution fusion | flops 2522087424 | bytes 21256192 | tf_op jit(solution)/shard_map/dot_general | solution.py:89
  368.4 3.3 collective-permute-start.1
  379.6 4.2 convolution_add_fusion
  397.9 3.8 fusion.62
  401.7 4.0 fusion.2
  406.6 4.4 fusion.148
  411.0 6.8 multiply_reduce_fusion.2
  417.8 7.0 multiply_convert_fusion.2
  429.0 20.1 %multiply_convert_fusion.3 = (bf16[512,3072]{1,0:T(8,128)(2,1)}, f32[512,3072]{1,0:T(8,128)}, f32[512,3072]{1,0:T(8,128)}) fusion(f32[3072]{0:T(1024)S(1)} %copy-done.132, bf16[1,768,3072]{2,1,0:T(8,128)(2,1)} %all-gather.21.cloned.1.call-done, bf16[512,768]{1,0:T(8,128)(2,1)S(1)} %copy-done.8, f32[768]{0:T(1024)S(1)} %convert_element_type.375, ...), kind=kOutput, calls=%fused_computation.45 | convolution fusion | flops 2522087424 | bytes 21256192 | tf_op jit(solution)/shard_map/dot_general | solution.py:89
  449.1 10.5 convert_reduce_fusion.2
  459.6 6.1 fusion.52
  465.7 3.1 fusion.249
  474.6 4.6 fusion.157
  479.2 5.2 fusion.233
  489.6 9.0 fusion.151
  498.6 9.6 multiply_reduce_fusion.1
  508.2 7.5 multiply_convert_fusion.1
  520.2 10.1 convert_reduce_fusion.1
  546.2 5.2 fusion.227
  557.3 4.4 add_add_fusion.9
  562.0 13.6 %multiply_reduce_fusion = (f32[12,512]{1,0:T(8,128)S(1)}, f32[12,512,512]{1,2,0:T(8,128)}) fusion(f32[12,512]{1,0:T(8,128)S(1)} %copy-done.89, f32[12,512,512]{1,2,0:T(8,128)} %copy-done, pred[512,512]{0,1:T(8,128)(4,1)S(1)} %copy-done.26, bf16[512,12,64]{0,2,1:T(8,128)(2,1)} %bitcast.349, bf16[512,12,64]{0,2,1:T(8,128)(2,1)} %bitcast.343), kind=kOutput, calls=%fused_computation.1 | convolution fusion | flops 418375680 | bytes 27049984 | tf_op jit(solution)/shard_map/thd,shd->hts/dot_general | solution.py:150
  575.7 7.1 multiply_convert_fusion
  587.3 3.2 fusion.154
  590.6 10.6 add_add_fusion.2
  601.9 5.0 fusion.230
  609.8 12.5 %convert_reduce_fusion = (f32[3072]{0:T(1024)S(1)}, bf16[512,3072]{1,0:T(8,128)(2,1)}) fusion(f32[512,3072]{1,0:T(8,128)} %get-tuple-element.80, bf16[512,768]{1,0:T(8,128)(2,1)} %copy-done.22, bf16[1,3072,768]{2,1,0:T(8,128)(2,1)} %all-gather.23.cloned.1.call-done, f32[512,3072]{1,0:T(8,128)} %get-tuple-element.160, f32[3072]{0:T(1024)S(1)} %copy-done.133), kind=kOutput, calls=%fused_computation.36 | convolution fusion | flops 2442654720 | bytes 21258240 | tf_op jit(solution)/shard_map/td,fd->tf/dot_general | solution.py:139
  622.3 9.1 add_add_fusion.1
  632.9 4.8 fusion.182
  640.5 6.8 add_add_fusion
  651.3 5.1 fusion.42
  663.5 5.2 fusion.48
  673.2 75.7 %all-reduce.15 = (f32[2304]{0:T(1024)S(1)}, f32[768]{0:T(1024)S(1)}, f32[3072]{0:T(1024)S(1)}, f32[768]{0:T(1024)S(1)}, f32[768]{0:T(1024)S(1)}, /*index=5*/f32[768]{0:T(1024)S(1)}, f32[768]{0:T(1024)S(1)}) all-reduce(f32[2304]{0:T(1024)S(1)} %add_add_fusion.12, ...), channel_id=18, replica_groups=mesh['section'=2,'dp'=16] {'dp'}, use_global_device_ids=true, to_apply=%region_43.44.clone | all-reduce | flops 9216 | bytes 73728
  752.5 3.4 select_bitcast_fusion.1
  757.8 87.7 %reduce-scatter.5.cloned.1.call-done = f32[48,2304]{1,0:T(8,128)} async-done(((f32[768,2304]{1,0:T(8,128)}), f32[48,2304]{1,0:T(8,128)}) %reduce-scatter.5.cloned.1.call-update) | async-done | bytes 442384 | tf_op jit(solution)/shard_map/reduce_scatter | solution.py:292
  845.5 176.9 %reduce-scatter.9.cloned.1.call-done = f32[48,3072]{1,0:T(8,128)} async-done(((f32[768,3072]{1,0:T(8,128)}), f32[48,3072]{1,0:T(8,128)}) %reduce-scatter.9.cloned.1.call-update) | async-done | bytes 589840 | tf_op jit(solution)/shard_map/reduce_scatter | solution.py:294
  1022.5 176.1 %reduce-scatter.11.cloned.1.call-done = f32[192,768]{1,0:T(8,128)} async-done(((f32[3072,768]{1,0:T(8,128)}), f32[192,768]{1,0:T(8,128)}) %reduce-scatter.11.cloned.1.call-update) | async-done | bytes 589840 | tf_op jit(solution)/shard_map/reduce_scatter | solution.py:295
  (524 shorter events, 165.4 us)
Async XLA Ops:
  7.2 102.1 %copy-start.2 = (bf16[2,512,768]{2,1,0:T(8,128)(2,1)S(1)}, bf16[2,512,768]{2,1,0:T(8,128)(2,1)}, u32[]{:S(2)}) copy-start(bf16[2,512,768]{2,1,0:T(8,128)(2,1)} %param.15) | copy-start | bytes 4718596
  7.2 102.0 %all-gather.17.cloned.1.call-start = ((), (), s32[]{:S(2)}) async-start(), calls=%async_computation.8 | async-start | bytes 3760128 | tf_op jit(solution)/shard_map/all_gather | solution.py:219
  7.9 160.0 %all-gather.21.cloned.1.call-start = ((), (), s32[]{:S(2)}) async-start(), calls=%async_computation.10 | async-start | bytes 5013504 | tf_op jit(solution)/shard_map/all_gather | solution.py:221
  8.7 241.1 %all-gather.23.cloned.1.call-start = ((), (), s32[]{:S(2)}) async-start(), calls=%async_computation.11 | async-start | bytes 5013504 | tf_op jit(solution)/shard_map/all_gather | solution.py:222
  9.4 297.8 %all-gather.19.cloned.1.call-start = ((), (), s32[]{:S(2)}) async-start(), calls=%async_computation.9 | async-start | bytes 1253376 | tf_op jit(solution)/shard_map/all_gather | solution.py:220
  10.0 747.9 %reduce-scatter.7.cloned.1.call-start = ((), (), s32[]{:S(2)}) async-start(), calls=%async_computation.5 | async-start | bytes 2506752 | tf_op jit(solution)/shard_map/reduce_scatter | solution.py:293
  99.9 328.5 %copy-start.62 = (f32[768]{0:T(1024)}, f32[768]{0:T(1024)S(1)}, u32[]{:S(2)}) copy-start(f32[768]{0:T(1024)S(1)} %convert_element_type.375) | copy-start | bytes 9220
  101.3 66.6 %copy-start.109 = (f32[512]{0:T(512)}, f32[512]{0:T(512)S(1)}, u32[]{:S(2)}) copy-start(f32[512]{0:T(512)S(1)} %broadcast_multiply_fusion.2) | copy-start | bytes 6148
  102.8 10.6 copy-start.115
  102.8 10.6 copy-start.134
  102.9 10.6 copy-start.111
  108.3 25.5 %copy-start.25 = (pred[512,512]{0,1:T(8,128)(4,1)}, pred[512,512]{0,1:T(8,128)(4,1)S(1)}, u32[]{:S(2)}) copy-start(pred[512,512]{0,1:T(8,128)(4,1)S(1)} %compare_and_fusion.2) | copy-start | bytes 786436
  109.2 17.1 %copy-start.96 = (f32[512,8]{0,1:T(8,128)}, f32[512,8]{0,1:T(8,128)S(1)}, u32[]{:S(2)}) copy-start(f32[512,8]{0,1:T(8,128)S(1)} %get-tuple-element.158) | copy-start | bytes 49156
  109.2 17.1 %copy-start.98 = (f32[512,8]{0,1:T(8,128)}, f32[512,8]{0,1:T(8,128)S(1)}, u32[]{:S(2)}) copy-start(f32[512,8]{0,1:T(8,128)S(1)} %get-tuple-element.159) | copy-start | bytes 49156
  109.2 221.4 %copy-start.100 = (f32[512,8]{0,1:T(8,128)}, f32[512,8]{0,1:T(8,128)S(1)}, u32[]{:S(2)}) copy-start(f32[512,8]{0,1:T(8,128)S(1)} %get-tuple-element.156) | copy-start | bytes 49156
  109.2 221.4 %copy-start.102 = (f32[512,8]{0,1:T(8,128)}, f32[512,8]{0,1:T(8,128)S(1)}, u32[]{:S(2)}) copy-start(f32[512,8]{0,1:T(8,128)S(1)} %get-tuple-element.157) | copy-start | bytes 49156
  135.8 32.1 %copy-start.116 = (f32[512]{0:T(512)S(1)}, f32[512]{0:T(512)}, u32[]{:S(2)}) copy-start(f32[512]{0:T(512)} %copy-done.115) | copy-start | bytes 6148
  135.8 32.1 %copy-start.130 = (f32[3072]{0:T(1024)S(1)}, f32[3072]{0:T(1024)}, u32[]{:S(2)}) copy-start(f32[3072]{0:T(1024)} %convert_element_type.376) | copy-start | bytes 36868
  139.4 167.9 %copy-start.66 = (bf16[12,64,512]{2,1,0:T(8,128)(2,1)}, bf16[12,64,512]{2,1,0:T(8,128)(2,1)S(1)}, u32[]{:S(2)}) copy-start(bf16[12,64,512]{2,1,0:T(8,128)(2,1)S(1)} %fusion.159) | copy-start | bytes 2359300
  249.8 57.4 %copy-start.139 = (f32[768]{0:T(1024)S(1)}, f32[768]{0:T(1024)}, u32[]{:S(2)}) copy-start(f32[768]{0:T(1024)} %convert_element_type.377) | copy-start | bytes 9220
  249.8 57.4 %copy-start.141 = (f32[768]{0:T(1024)S(1)}, f32[768]{0:T(1024)}, u32[]{:S(2)}) copy-start(f32[768]{0:T(1024)} %convert_element_type.373) | copy-start | bytes 9220
  310.1 3.3 collective-permute-start
  312.3 25.8 %copy-start.27 = (pred[512,512]{0,1:T(8,128)(4,1)}, pred[512,512]{0,1:T(8,128)(4,1)S(1)}, u32[]{:S(2)}) copy-start(pred[512,512]{0,1:T(8,128)(4,1)S(1)} %compare_and_fusion.1) | copy-start | bytes 786436
  313.8 30.1 %copy-start.10 = (bf16[512,768]{1,0:T(8,128)(2,1)}, bf16[512,768]{1,0:T(8,128)(2,1)S(1)}, u32[]{:S(2)}) copy-start(bf16[512,768]{1,0:T(8,128)(2,1)S(1)} %get-tuple-element.78) | copy-start | bytes 2359300
  313.8 30.1 %copy-start.90 = (f32[512]{0:T(512)}, f32[512]{0:T(512)S(1)}, u32[]{:S(2)}) copy-start(f32[512]{0:T(512)S(1)} %broadcast_multiply_fusion.1) | copy-start | bytes 6148
  314.2 29.7 %copy-start.94 = (f32[512]{0:T(512)}, f32[512]{0:T(512)S(1)}, u32[]{:S(2)}) copy-start(f32[512]{0:T(512)S(1)} %fusion.191) | copy-start | bytes 6148
  320.7 17.5 %copy-start.30 = (bf16[512,768]{0,1:T(8,128)(2,1)}, bf16[512,768]{0,1:T(8,128)(2,1)S(1)}, u32[]{:S(2)}) copy-start(bf16[512,768]{0,1:T(8,128)(2,1)S(1)} %copy.123) | copy-start | bytes 2359300
  340.1 23.7 %slice-start.8 = ((s8[4718592]{0:T(1024)(128)(4,1)}), s8[4194304]{0:T(1024)(128)(4,1)S(1)}, s32[]{:S(2)}) async-start(s8[4718592]{0:T(1024)(128)(4,1)} %bitcast.389), calls=%async_computation.20 | async-start | bytes 8388608
  343.9 22.6 %copy-start.71 = (bf16[12,64,512]{2,1,0:T(8,128)(2,1)}, bf16[12,64,512]{2,1,0:T(8,128)(2,1)S(1)}, u32[]{:S(2)}) copy-start(bf16[12,64,512]{2,1,0:T(8,128)(2,1)S(1)} %fusion.158) | copy-start | bytes 2359300
  343.9 19.8 %slice-start.9 = ((s8[4718592]{0:T(1024)(128)(4,1)}), s8[524288]{0:T(1024)(128)(4,1)S(1)}, s32[]{:S(2)}) async-start(s8[4718592]{0:T(1024)(128)(4,1)} %bitcast.389), calls=%async_computation.21 | async-start | bytes 1048576
  368.4 10.4 collective-permute-start.1
  428.3 50.8 %copy-start.36 = (bf16[512,12,64]{0,2,1:T(8,128)(2,1)}, bf16[512,12,64]{0,2,1:T(8,128)(2,1)S(1)}, u32[]{:S(2)}) copy-start(bf16[512,12,64]{0,2,1:T(8,128)(2,1)S(1)} %pad_maximum_fusion.10) | copy-start | bytes 2359300
  429.0 50.1 %copy-start.38 = (bf16[512,12,64]{0,2,1:T(8,128)(2,1)}, bf16[512,12,64]{0,2,1:T(8,128)(2,1)S(1)}, u32[]{:S(2)}) copy-start(bf16[512,12,64]{0,2,1:T(8,128)(2,1)S(1)} %pad_maximum_fusion.9) | copy-start | bytes 2359300
  473.1 11.2 collective-permute-start.2
  489.6 18.6 %slice-start.3 = ((s8[12582912]{0:T(1024)(128)(4,1)}), s8[4194304]{0:T(1024)(128)(4,1)S(1)}, s32[]{:S(2)}) async-start(s8[12582912]{0:T(1024)(128)(4,1)} %bitcast.323), calls=%async_computation.15 | async-start | bytes 8388608
  489.6 18.6 %slice-start.4 = ((s8[12582912]{0:T(1024)(128)(4,1)}), s8[4194304]{0:T(1024)(128)(4,1)S(1)}, s32[]{:S(2)}) async-start(s8[12582912]{0:T(1024)(128)(4,1)} %bitcast.323), calls=%async_computation.16 | async-start | bytes 8388608
  519.2 11.1 slice-start.6
  519.5 26.8 %copy-start.40 = (bf16[512,12,64]{0,2,1:T(8,128)(2,1)}, bf16[512,12,64]{0,2,1:T(8,128)(2,1)S(1)}, u32[]{:S(2)}) copy-start(bf16[512,12,64]{0,2,1:T(8,128)(2,1)S(1)} %pad_maximum_fusion.12) | copy-start | bytes 2359300
  519.5 26.7 %copy-start.42 = (bf16[512,12,64]{0,2,1:T(8,128)(2,1)}, bf16[512,12,64]{0,2,1:T(8,128)(2,1)S(1)}, u32[]{:S(2)}) copy-start(bf16[512,12,64]{0,2,1:T(8,128)(2,1)S(1)} %pad_maximum_fusion.11) | copy-start | bytes 2359300
  540.2 11.2 collective-permute-start.3
  561.7 283.8 %reduce-scatter.5.cloned.1.call-start = ((), (), s32[]{:S(2)}) async-start(), calls=%async_computation.4 | async-start | bytes 7520256 | tf_op jit(solution)/shard_map/reduce_scatter | solution.py:292
  562.0 13.7 %slice-start = ((s8[12582912]{0:T(1024)(128)(4,1)}), s8[4194304]{0:T(1024)(128)(4,1)S(1)}, s32[]{:S(2)}) async-start(s8[12582912]{0:T(1024)(128)(4,1)} %bitcast.321), calls=%async_computation.12 | async-start | bytes 8388608
  562.0 13.7 %slice-start.1 = ((s8[12582912]{0:T(1024)(128)(4,1)}), s8[4194304]{0:T(1024)(128)(4,1)S(1)}, s32[]{:S(2)}) async-start(s8[12582912]{0:T(1024)(128)(4,1)} %bitcast.321), calls=%async_computation.13 | async-start | bytes 8388608
  562.0 13.7 %slice-start.2 = ((s8[12582912]{0:T(1024)(128)(4,1)}), s8[4194304]{0:T(1024)(128)(4,1)S(1)}, s32[]{:S(2)}) async-start(s8[12582912]{0:T(1024)(128)(4,1)} %bitcast.321), calls=%async_computation.14 | async-start | bytes 8388608
  590.5 10.7 copy-start.50
  601.3 421.2 %reduce-scatter.9.cloned.1.call-start = ((), (), s32[]{:S(2)}) async-start(), calls=%async_computation.6 | async-start | bytes 10027008 | tf_op jit(solution)/shard_map/reduce_scatter | solution.py:294
  631.5 567.1 %reduce-scatter.11.cloned.1.call-start = ((), (), s32[]{:S(2)}) async-start(), calls=%async_computation.7 | async-start | bytes 10027008 | tf_op jit(solution)/shard_map/reduce_scatter | solution.py:295
  748.9 449.7 %copy-start.154 = (f32[1,48]{1,0:T(1,128)}, f32[1,48]{1,0:T(1,128)S(1)}, u32[]{:S(2)}) copy-start(f32[1,48]{1,0:T(1,128)S(1)} %dynamic-slice_bitcast_fusion.4) | copy-start | bytes 580
  (132 other events, 474.6 us)
Sparse Core Ops, SparseCore 0:
  10.8 74.8 all-gather.16
  88.5 79.3 all-gather.20
  170.7 79.0 all-gather.22
  252.5 54.7 all-gather.18
  561.9 127.2 reduce-scatter.6
  695.8 149.7 reduce-scatter.4
  852.7 169.6 reduce-scatter.8
  1028.7 169.8 reduce-scatter.10
where the time goes:
time: 1220 us; the launch traced here: 1210 us
  waiting for transfers between devices  585 us (48%)
  matrix products  294 us (24%)
  blocking collectives  155 us (13%)
  local copies, waits for them, and re-layouts  73.9 us (6%)
  other arithmetic  68.9 us (6%)
  between operations  20.8 us (2%)
    reduce_scatter x1, waiting for transfers between devices, on_device(): lax.psum_scatter(totals[2], 'dp', scatter_dimension=0, tiled=True)  177 us
    reduce_scatter x1, waiting for transfers between devices, on_device(): lax.psum_scatter(totals[3], 'dp', scatter_dimension=0, tiled=True)  176 us
    unnamed x2, blocking collectives  155 us
    reduce_scatter x1, waiting for transfers between devices, on_device(): lax.psum_scatter(totals[0], 'dp', scatter_dimension=0, tiled=True)  87.7 us
    all_gather x1, waiting for transfers between devices, on_device(): lax.all_gather(down_weight[0], 'dp', axis=0, tiled=True)  61.9 us
    dot_general x3, matrix products, layer_forward(): jnp.dot(normed_m, up_w, preferred_element_type=jnp.float32)  59.9 us
    all_gather x1, waiting for transfers between devices, on_device(): lax.all_gather(out_weight[0], 'dp', axis=0, tiled=True)  50.4 us
    dot_general x3, matrix products, layer_backward(): jnp.einsum('td,fd->tf', up_low, down_w, preferred_element_type=jnp.float32)  33 us
  transfers between devices with their start and end apart: 12, of which 7 were waited for; matrix products, arithmetic and copies ran while one was open for 17% of the time, Pallas kernels for 0%

commit v1 on v0

--- a/solution.py
+++ b/solution.py
@@ -5,12 +5,6 @@
 
 EPSILON = 1e-05
 HEAD_WIDTH = 64
-
-
-def from_behind(value, axis, steps):
-    count = lax.axis_size(axis)
-    first, last = (max(0, -steps), min(count, count - steps))
-    return lax.ppermute(value, axis, [(source, source + steps) for source in range(first, last)])
 
 
 def layer_norm(values, gain, offset):
@@ -67,15 +61,18 @@
     normed_m = layer_norm(entry, gain_m.astype(jnp.float32), shift_m.astype(jnp.float32)).astype(
         jnp.bfloat16
     )
-    qkv = jnp.dot(normed_a, qkv_w, preferred_element_type=jnp.float32) + qkv_b.astype(jnp.float32)
+    query, key, value = (
+        jnp.dot(normed_a, part, preferred_element_type=jnp.float32) + bias.astype(jnp.float32)
+        for part, bias in zip(qkv_w, jnp.split(qkv_b, 3))
+    )
     cosine, sine = angle_tables(positions)
-    queries = rotate(qkv[:, :width].reshape(count, heads, HEAD_WIDTH), cosine, sine).astype(
+    queries = rotate(query.reshape(count, heads, HEAD_WIDTH), cosine, sine).astype(
         jnp.bfloat16
     )
-    keys = rotate(qkv[:, width : 2 * width].reshape(count, heads, HEAD_WIDTH), cosine, sine).astype(
+    keys = rotate(key.reshape(count, heads, HEAD_WIDTH), cosine, sine).astype(
         jnp.bfloat16
     )
-    values = qkv[:, 2 * width :].reshape(count, heads, HEAD_WIDTH).astype(jnp.bfloat16)
+    values = value.reshape(count, heads, HEAD_WIDTH).astype(jnp.bfloat16)
     allowed = (seq_ids[:, None] == seq_ids[None, :]) & (positions[:, None] >= positions[None, :])
     scores = jnp.einsum("thd,shd->hts", queries, keys, preferred_element_type=jnp.float32) * 0.125
     scores = jnp.where(allowed[None], scores, -1e30)
@@ -159,17 +156,19 @@
     d_keys = (
         jnp.einsum("hts,thd->shd", d_scores, queries, preferred_element_type=jnp.float32) * 0.125
     )
-    d_qkv = jnp.concatenate(
-        [
-            unrotate(d_queries, cosine, sine).reshape(count, width),
-            unrotate(d_keys, cosine, sine).reshape(count, width),
-            d_values.reshape(count, width),
-        ],
-        axis=1,
-    ).astype(jnp.bfloat16)
-    grad_qkv_w = jnp.einsum("td,te->de", normed_a, d_qkv, preferred_element_type=jnp.float32)
-    grad_qkv_b = jnp.sum(d_qkv.astype(jnp.float32), axis=0)
-    d_normed_a = jnp.einsum("te,de->td", d_qkv, qkv_w, preferred_element_type=jnp.float32)
+    d_qkv = [
+        part.reshape(count, width).astype(jnp.bfloat16)
+        for part in (unrotate(d_queries, cosine, sine), unrotate(d_keys, cosine, sine), d_values)
+    ]
+    grad_qkv_w = [
+        jnp.einsum("td,te->de", normed_a, part, preferred_element_type=jnp.float32)
+        for part in d_qkv
+    ]
+    grad_qkv_b = jnp.concatenate([jnp.sum(part.astype(jnp.float32), axis=0) for part in d_qkv])
+    d_normed_a = sum(
+        jnp.einsum("te,de->td", part, weight, preferred_element_type=jnp.float32)
+        for part, weight in zip(d_qkv, qkv_w)
+    )
     _, norm_back_a = jax.vjp(
         layer_norm, entry, gain_a.astype(jnp.float32), shift_a.astype(jnp.float32)
     )
@@ -194,6 +193,72 @@
         grad_shift_m,
     )
     return (d_entry, grads)
+
+
+VECTOR_ROWS = 16
+
+
+def swap(value):
+    return lax.ppermute(value, "section", [(0, 1), (1, 0)])
+
+
+def column_blocks(shard, width):
+    return jnp.concatenate(jnp.split(shard, shard.shape[1] // width, axis=1), axis=0)
+
+
+def both_halves(own, core):
+    other = swap(own)
+    return (jnp.where(core == 0, own, other), jnp.where(core == 0, other, own))
+
+
+def unpack(gathered, core, width, units):
+    attn, mlp = gathered
+    count = attn.shape[0]
+    rows = width // count
+    first, second = both_halves(attn, core)
+    up, down = both_halves(mlp, core)
+    square = lambda block: block.reshape(width, width)
+    query, key = square(first[:, :rows]), square(first[:, rows : 2 * rows])
+    value, out = square(second[:, :rows]), square(second[:, rows : 2 * rows])
+    vectors = first[:, 2 * rows :].reshape(count, -1)
+    small, at = [], 0
+    for size in units:
+        small.append(vectors[:, at : at + size * rows].reshape(size * width))
+        at += size * rows
+    up = up.reshape(count, -1, rows, width).transpose(0, 2, 1, 3).reshape(width, -1)
+    down = down.reshape(-1, width)
+    return ((query, key, value), out, up, down, *small)
+
+
+def pack_vectors(vectors, count, width):
+    flat = jnp.concatenate([vector.reshape(count, -1) for vector in vectors], axis=1)
+    flat = jnp.pad(flat, ((0, 0), (0, VECTOR_ROWS * width - flat.shape[1])))
+    return flat.reshape(count, VECTOR_ROWS, width)
+
+
+def reduce_pair(low, high, core):
+    arrived = swap(jnp.where(core == 0, high, low))
+    own = jnp.where(core == 0, low, high)
+    total = (own.astype(jnp.float32) + arrived.astype(jnp.float32)).astype(jnp.bfloat16)
+    return lax.psum_scatter(total, "dp", scatter_dimension=0, tiled=False)
+
+
+def reduce_mlp(grads, core, count, width):
+    rows = width // count
+    up = grads[2].astype(jnp.bfloat16).reshape(count, rows, -1, width)
+    up = up.transpose(0, 2, 1, 3).reshape(count, -1, width)
+    down = grads[3].astype(jnp.bfloat16).reshape(count, -1, width)
+    return reduce_pair(up, down, core)
+
+
+def reduce_attn(grads, core, count, width):
+    rows = width // count
+    query, key, value = (part.astype(jnp.bfloat16).reshape(count, rows, width) for part in grads[0])
+    out = grads[1].astype(jnp.bfloat16).reshape(count, rows, width)
+    small = pack_vectors([vector.astype(jnp.bfloat16) for vector in grads[4:]], count, width)
+    low = jnp.concatenate([query, key, small], axis=1)
+    high = jnp.concatenate([value, out, jnp.zeros_like(small)], axis=1)
+    return reduce_pair(low, high, core)
 
 
 def on_device(
@@ -213,95 +278,80 @@
     mlp_gain,
     mlp_shift,
 ):
-    section_index = lax.axis_index("section")
-    batches = tokens.shape[0]
-    gathered = (
-        lax.all_gather(qkv_weight[0], "dp", axis=0, tiled=True),
-        lax.all_gather(out_weight[0], "dp", axis=0, tiled=True),
-        lax.all_gather(up_weight[0], "dp", axis=0, tiled=True),
-        lax.all_gather(down_weight[0], "dp", axis=0, tiled=True),
-        lax.all_gather(qkv_bias[0], "dp", axis=0, tiled=True),
-        lax.all_gather(out_bias[0], "dp", axis=0, tiled=True),
-        lax.all_gather(up_bias[0], "dp", axis=0, tiled=True),
-        lax.all_gather(down_bias[0], "dp", axis=0, tiled=True),
-        lax.all_gather(attn_gain[0], "dp", axis=0, tiled=True),
-        lax.all_gather(attn_shift[0], "dp", axis=0, tiled=True),
-        lax.all_gather(mlp_gain[0], "dp", axis=0, tiled=True),
-        lax.all_gather(mlp_shift[0], "dp", axis=0, tiled=True),
-    )
-    received = jnp.zeros(tokens.shape[1:], jnp.bfloat16)
+    core = lax.axis_index("section")
+    count = lax.axis_size("dp")
+    width = tokens.shape[2]
+    rows = width // count
+    vectors = (
+        qkv_bias[0],
+        out_bias[0],
+        up_bias[0],
+        down_bias[0],
+        attn_gain[0],
+        attn_shift[0],
+        mlp_gain[0],
+        mlp_shift[0],
+    )
+    units = [vector.shape[0] // rows for vector in vectors]
+    qkv_blocks = column_blocks(qkv_weight[0], width)
+    small = pack_vectors([vector[None] for vector in vectors], 1, width)[0]
+    attn_low = jnp.concatenate([qkv_blocks[: 2 * rows], small], axis=0)
+    attn_high = jnp.concatenate(
+        [qkv_blocks[2 * rows :], out_weight[0], jnp.zeros_like(small)], axis=0
+    )
+    mlp_low = column_blocks(up_weight[0], width)
+    mlp_high = down_weight[0]
+    pieces = []
+    for low, high in ((attn_low, attn_high), (mlp_low, mlp_high)):
+        arrived = swap(jnp.where(core == 0, high, low))
+        own = jnp.where(core == 0, low, high)
+        pieces.append((jnp.where(core == 0, own, arrived), jnp.where(core == 0, arrived, own)))
+    gathered = [
+        tuple(lax.all_gather(piece[layer], "dp", axis=0, tiled=False) for piece in pieces)
+        for layer in range(2)
+    ]
+    parameters = [unpack(gathered[layer], core, width, units) for layer in range(2)]
+
+    seq_lengths = lax.dynamic_index_in_dim(lengths, core, 0, keepdims=False)[0]
+    entry = lax.dynamic_index_in_dim(tokens, core, 0, keepdims=False).astype(jnp.float32)
     entries, keeps, results = ([], [], [])
-    for moment in range(batches + 1):
-        batch_index = jnp.clip(moment - section_index, 0, batches - 1)
-        own_tokens = lax.dynamic_index_in_dim(tokens, batch_index, 0, keepdims=False)
-        entry = jnp.where(section_index == 0, own_tokens, received).astype(jnp.float32)
-        seq_lengths = lax.dynamic_index_in_dim(lengths, batch_index, 0, keepdims=False)[0]
-        result, kept = layer_forward(entry, seq_lengths, gathered)
+    for layer in range(2):
+        result, kept = layer_forward(entry, seq_lengths, parameters[layer])
         rounded = result.astype(jnp.bfloat16)
         entries.append(entry)
         keeps.append(kept)
         results.append(rounded)
-        if moment < batches:
-            received = from_behind(rounded, "section", 1)
-    layer_outputs = jnp.stack(
-        [
-            jnp.where(section_index == 0, results[batch], results[batch + 1])
-            for batch in range(batches)
-        ]
-    )
-    gathered = (
-        lax.all_gather(qkv_weight[0], "dp", axis=0, tiled=True),
-        lax.all_gather(out_weight[0], "dp", axis=0, tiled=True),
-        lax.all_gather(up_weight[0], "dp", axis=0, tiled=True),
-        lax.all_gather(down_weight[0], "dp", axis=0, tiled=True),
-        lax.all_gather(qkv_bias[0], "dp", axis=0, tiled=True),
-        lax.all_gather(out_bias[0], "dp", axis=0, tiled=True),
-        lax.all_gather(up_bias[0], "dp", axis=0, tiled=True),
-        lax.all_gather(down_bias[0], "dp", axis=0, tiled=True),
-        lax.all_gather(attn_gain[0], "dp", axis=0, tiled=True),
-        lax.all_gather(attn_shift[0], "dp", axis=0, tiled=True),
-        lax.all_gather(mlp_gain[0], "dp", axis=0, tiled=True),
-        lax.all_gather(mlp_shift[0], "dp", axis=0, tiled=True),
-    )
-    arriving = jnp.zeros(tokens.shape[1:], jnp.float32)
-    totals = None
-    backs = []
-    for moment in range(batches + 1):
-        forward_moment = batches - moment
-        batch_number = forward_moment - section_index
-        batch_index = jnp.clip(batch_number, 0, batches - 1)
-        live_flag = ((batch_number >= 0) & (batch_number < batches)).astype(jnp.float32)
-        own_grad = lax.dynamic_index_in_dim(cotangent, batch_index, 0, keepdims=False).astype(
-            jnp.float32
+        entry = rounded.astype(jnp.float32)
+
+    def by_layer(first, second):
+        own = jnp.where(core == 0, first, second)
+        arrived = swap(jnp.where(core == 0, second, first))
+        return jnp.stack(
+            [jnp.where(core == 0, own, arrived), jnp.where(core == 0, arrived, own)]
         )
-        upstream = jnp.where(section_index == 1, own_grad, arriving) * live_flag
-        d_entry, grads = layer_backward(
-            upstream, entries[forward_moment], keeps[forward_moment], gathered
-        )
-        totals = grads if totals is None else jax.tree.map(jnp.add, totals, grads)
-        backs.append(d_entry)
-        if moment < batches:
-            arriving = from_behind(d_entry.astype(jnp.bfloat16), "section", -1).astype(jnp.float32)
-    input_grads = jnp.stack(
-        [
-            jnp.where(section_index == 0, backs[batches - batch], backs[batches - 1 - batch])
-            for batch in range(batches)
-        ]
-    )
-    reduced = (
-        lax.psum_scatter(totals[0], "dp", scatter_dimension=0, tiled=True),
-        lax.psum_scatter(totals[1], "dp", scatter_dimension=0, tiled=True),
-        lax.psum_scatter(totals[2], "dp", scatter_dimension=0, tiled=True),
-        lax.psum_scatter(totals[3], "dp", scatter_dimension=0, tiled=True),
-        lax.psum_scatter(totals[4], "dp", scatter_dimension=0, tiled=True),
-        lax.psum_scatter(totals[5], "dp", scatter_dimension=0, tiled=True),
-        lax.psum_scatter(totals[6], "dp", scatter_dimension=0, tiled=True),
-        lax.psum_scatter(totals[7], "dp", scatter_dimension=0, tiled=True),
-        lax.psum_scatter(totals[8], "dp", scatter_dimension=0, tiled=True),
-        lax.psum_scatter(totals[9], "dp", scatter_dimension=0, tiled=True),
-        lax.psum_scatter(totals[10], "dp", scatter_dimension=0, tiled=True),
-        lax.psum_scatter(totals[11], "dp", scatter_dimension=0, tiled=True),
-    )
+
+    layer_outputs = by_layer(*results)
+    upstream = lax.dynamic_index_in_dim(cotangent, core, 0, keepdims=False).astype(jnp.float32)
+    backs, mlps, attns = ([None, None], [None, None], [None, None])
+    for layer in (1, 0):
+        d_entry, grads = layer_backward(upstream, entries[layer], keeps[layer], parameters[layer])
+        backs[layer] = d_entry
+        mlps[layer] = reduce_mlp(grads, core, count, width)
+        attns[layer] = reduce_attn(grads, core, count, width)
+        upstream = d_entry.astype(jnp.bfloat16).astype(jnp.float32)
+    input_grads = by_layer(*backs)
+    mlp_low, mlp_high = by_layer(*mlps).astype(jnp.float32)
+    attn_low, attn_high = by_layer(*attns).astype(jnp.float32)
+    grad_qkv = jnp.concatenate(
+        [attn_low[:rows], attn_low[rows : 2 * rows], attn_high[:rows]], axis=1
+    )
+    grad_out = attn_high[rows : 2 * rows]
+    grad_up = jnp.concatenate(jnp.split(mlp_low, mlp_low.shape[0] // rows, axis=0), axis=1)
+    flat = attn_low[2 * rows :].reshape(-1)
+    reduced, at = [grad_qkv, grad_out, grad_up, mlp_high], 0
+    for size in units:
+        reduced.append(flat[at : at + size * rows])
+        at += size * rows
     return (layer_outputs[None], input_grads[None]) + tuple((piece[None] for piece in reduced))
 
 

time: 1220 us -> 1120 us (0.918)
  blocking collectives: 155 us -> 0 us
  waiting for transfers between devices: 585 us -> 703 us
  matrix products: 294 us -> 198 us
  other arithmetic: 68.9 us -> 97.8 us
  local copies, waits for them, and re-layouts: 73.9 us -> 94.4 us
    unnamed x2 -> x0, blocking collectives: 155 us -> none
    all_gather x4, waiting for transfers between devices: 141 us -> 227 us  [on_device(): lax.all_gather(piece[layer], 'dp', axis=0, tiled=False)]
    select_n x0 -> x14, other arithmetic: none -> 38.7 us  [the longest x4 22.1 us: both_halves(): return (jnp.where(core == 0, own, other), jnp.where(core == 0, other, own))]
    ppermute x4 -> x14, waiting for transfers between devices: 1.12 us -> 30.6 us  [swap(): return lax.ppermute(value, 'section', [(0, 1), (1, 0)])]
    reshape x0 -> x11, local copies, waits for them, and re-layouts: none -> 25.5 us  [the longest x2 19.5 us: reduce_mlp(): up = grads[2].astype(jnp.bfloat16).reshape(count, rows, -1, width)]
    dot_general x3 -> x2, matrix products: 59.9 us -> 39.6 us  [layer_forward(): jnp.dot(normed_m, up_w, preferred_element_type=jnp.float32)]
    convert_element_type x9 -> x7, other arithmetic: 5.32 us -> 20.5 us  [the longest x3 19.6 us: reduce_pair(): (own.astype(jnp.float32) + arrived.astype(jnp.float32)).astype(jnp.bfloat16)]
    slice x15 -> x11, local copies, waits for them, and re-layouts: 29.2 us -> 14.2 us  [the longest x2 7.42 us: unpack(): query, key = (square(first[:, :rows]), square(first[:, rows:2 * rows]))]
  transfers between devices with their start and end apart: 12 -> 22, of which waited for: 7 -> 16; matrix products, arithmetic and copies ran while one was open for 17% -> 21% of each run, Pallas kernels for 0% -> 0%
where the time goes in v1:
time: 1120 us; the launch traced here: 1110 us
  waiting for transfers between devices  703 us (63%)
  matrix products  198 us (18%)
  other arithmetic  97.8 us (9%)
  local copies, waits for them, and re-layouts  94.4 us (8%)
  between operations  16.1 us (1%)
    reduce_scatter x4, waiting for transfers between devices, reduce_pair(): return lax.psum_scatter(total, 'dp', scatter_dimension=0, tiled=False)  445 us
    all_gather x4, waiting for transfers between devices, on_device(): lax.all_gather(piece[layer], 'dp', axis=0, tiled=False)  227 us
    dot_general x2, matrix products, layer_forward(): jnp.dot(normed_m, up_w, preferred_element_type=jnp.float32)  39.6 us
    ppermute x14, waiting for transfers between devices, swap(): return lax.ppermute(value, 'section', [(0, 1), (1, 0)])  30.6 us
  transfers between devices with their start and end apart: 22, of which 16 were waited for; matrix products, arithmetic and copies ran while one was open for 21% of the time, Pallas kernels for 0%

profile of v1, /device:TPU:0, one launch (start us, length us, event | category | flops | bytes accessed | tf_op | source)
XLA Modules:
  0.0 1114.8 jit_solution(17152067107972964812)
XLA Ops:
  18.4 63.0 %all-gather.9.cloned.1.call-done = bf16[1792,768]{1,0:T(8,128)(2,1)} async-done(((bf16[112,768]{1,0:T(8,128)(2,1)}), bf16[1792,768]{1,0:T(8,128)(2,1)}) %all-gather.9.cloned.1.call-update) | async-done | bytes 2752528 | tf_op jit(solution)/shard_map/all_gather | solution.py:310
  82.7 65.9 %all-gather.13.cloned.1.call-done = bf16[1792,768]{1,0:T(8,128)(2,1)} async-done(((bf16[112,768]{1,0:T(8,128)(2,1)}), bf16[1792,768]{1,0:T(8,128)(2,1)}) %all-gather.13.cloned.1.call-update) | async-done | bytes 2752528 | tf_op jit(solution)/shard_map/all_gather | solution.py:310
  151.2 4.5 broadcast_select_fusion.9
  173.0 3.3 convolution_add_fusion.2
  179.3 4.5 broadcast_select_fusion.7
  196.3 34.7 %all-gather.11.cloned.1.call-done = bf16[3072,768]{1,0:T(8,128)(2,1)} async-done(((bf16[192,768]{1,0:T(8,128)(2,1)}), bf16[3072,768]{1,0:T(8,128)(2,1)}) %all-gather.11.cloned.1.call-update) | async-done | bytes 4718608 | tf_op jit(solution)/shard_map/all_gather | solution.py:310
  232.1 3.4 fusion.24
  238.9 4.6 fusion.174
  243.4 3.8 fusion.81
  250.1 63.3 %all-gather.15.cloned.1.call-done = bf16[3072,768]{1,0:T(8,128)(2,1)} async-done(((bf16[192,768]{1,0:T(8,128)(2,1)}), bf16[3072,768]{1,0:T(8,128)(2,1)}) %all-gather.15.cloned.1.call-update) | async-done | bytes 4718608 | tf_op jit(solution)/shard_map/all_gather | solution.py:310
  313.3 6.5 broadcast_select_fusion.2
  323.6 18.4 %multiply_convert_fusion.3 = (bf16[512,3072]{1,0:T(8,128)(2,1)S(1)}, f32[512,3072]{1,0:T(8,128)}, f32[512,3072]{1,0:T(8,128)}) fusion(f32[3072]{0:T(1024)S(1)} %reshape.912, bf16[768,3072]{1,0:T(8,128)(2,1)S(1)} %bitcast.327, f32[768]{0:T(1024)S(1)} %reshape.911, f32[768]{0:T(1024)S(1)} %reshape.910, f32[512]{0:T(512)S(1)} %fusion.116, ...), kind=kOutput, calls=%fused_computation.41 | convolution fusion | flops 2522087424 | bytes 21258244 | tf_op jit(solution)/shard_map/dot_general | solution.py:86
  351.8 3.5 convolution_add_fusion
  365.1 3.4 fusion.25
  371.2 7.2 multiply_reduce_fusion.1
  378.4 7.0 multiply_convert_fusion.1
  390.5 3.8 fusion.80
  405.6 4.0 bitcast_reduce_fusion.1
  409.6 6.6 broadcast_select_fusion
  421.9 21.2 %multiply_convert_fusion.2 = (bf16[512,3072]{1,0:T(8,128)(2,1)}, f32[512,3072]{1,0:T(8,128)}, f32[512,3072]{1,0:T(8,128)}) fusion(f32[3072]{0:T(1024)S(1)} %copy-done.90, bf16[768,3072]{1,0:T(8,128)(2,1)S(1)} %bitcast.329, bf16[512,768]{1,0:T(8,128)(2,1)S(1)} %get-tuple-element.166, f32[768]{0:T(1024)S(1)} %copy-done.98, f32[768]{0:T(1024)S(1)} %copy-done.76, ...), kind=kOutput, calls=%fused_computation.28 | convolution fusion | flops 2522087424 | bytes 21256192 | tf_op jit(solution)/shard_map/dot_general | solution.py:86
  443.1 9.5 fusion.181
  452.6 4.7 fusion.186
  460.4 5.1 convert_reduce_fusion.2
  470.5 7.6 bitcast_reduce_fusion
  482.4 10.2 multiply_reduce_fusion
  492.6 7.2 multiply_convert_fusion
  513.6 9.6 fusion.180
  524.1 9.7 fusion.48
  534.4 6.2 broadcast_select_fusion.5
  541.2 4.6 collective-permute-done.8
  545.9 3.9 collective-permute-done.9
  549.9 4.6 add_convert_fusion.5
  555.1 6.5 convolution_convert_fusion.1
  561.6 9.8 reshape.903
  571.4 3.4 copy.94
  578.2 3.6 bitcast_select_fusion
  582.3 7.8 collective-permute-done.12
  590.2 8.3 add_convert_fusion
  599.9 6.7 convolution_convert_fusion.3
  606.6 9.8 reshape.900
  616.4 3.4 copy.93
  625.8 7.7 collective-permute-done.11
  633.5 6.7 add_convert_fusion.1
  646.1 3.5 collective-permute-done.6
  651.8 31.3 %reduce-scatter.5.cloned.1.call-done = bf16[1,112,768]{2,1,0:T(8,128)(2,1)} async-done(((bf16[16,112,768]{2,1,0:T(8,128)(2,1)}), bf16[1,112,768]{2,1,0:T(8,128)(2,1)}) %reduce-scatter.5.cloned.1.call-update) | async-done | bytes 172048 | tf_op jit(solution)/shard_map/reduce_scatter | solution.py:243
  683.1 134.6 %reduce-scatter.7.cloned.1.call-done = bf16[1,112,768]{2,1,0:T(8,128)(2,1)} async-done(((bf16[16,112,768]{2,1,0:T(8,128)(2,1)}), bf16[1,112,768]{2,1,0:T(8,128)(2,1)}) %reduce-scatter.7.cloned.1.call-update) | async-done | bytes 172048 | tf_op jit(solution)/shard_map/reduce_scatter | solution.py:243
  823.2 136.3 %reduce-scatter.11.cloned.1.call-done = bf16[1,192,768]{2,1,0:T(8,128)(2,1)} async-done(((bf16[16,192,768]{2,1,0:T(8,128)(2,1)}), bf16[1,192,768]{2,1,0:T(8,128)(2,1)}) %reduce-scatter.11.cloned.1.call-update) | async-done | bytes 294928 | tf_op jit(solution)/shard_map/reduce_scatter | solution.py:243
  959.5 142.7 %reduce-scatter.9.cloned.1.call-done = bf16[1,192,768]{2,1,0:T(8,128)(2,1)} async-done(((bf16[16,192,768]{2,1,0:T(8,128)(2,1)}), bf16[1,192,768]{2,1,0:T(8,128)(2,1)}) %reduce-scatter.9.cloned.1.call-update) | async-done | bytes 294928 | tf_op jit(solution)/shard_map/reduce_scatter | solution.py:243
  (460 shorter events, 161.0 us)
Async XLA Ops:
  7.2 74.2 %copy-start.106 = (s32[2,1,4]{2,1,0:T(1,128)S(1)}, s32[2,1,4]{2,1,0:T(1,128)}, u32[]{:S(2)}) copy-start(s32[2,1,4]{2,1,0:T(1,128)} %param.16) | copy-start | bytes 100
  7.2 74.2 %all-gather.9.cloned.1.call-start = ((), (), s32[]{:S(2)}) async-start(), calls=%async_computation.8 | async-start | bytes 2924544 | tf_op jit(solution)/shard_map/all_gather | solution.py:310
  7.3 74.3 %copy-start.22 = (bf16[2,512,768]{2,1,0:T(8,128)(2,1)S(1)}, bf16[2,512,768]{2,1,0:T(8,128)(2,1)}, u32[]{:S(2)}) copy-start(bf16[2,512,768]{2,1,0:T(8,128)(2,1)} %param.15) | copy-start | bytes 4718596
  10.4 1.6 collective-permute-start
  13.8 134.8 %all-gather.13.cloned.1.call-start = ((), (), s32[]{:S(2)}) async-start(), calls=%async_computation.10 | async-start | bytes 2924544 | tf_op jit(solution)/shard_map/all_gather | solution.py:310
  14.5 216.4 %all-gather.11.cloned.1.call-start = ((), (), s32[]{:S(2)}) async-start(), calls=%async_computation.9 | async-start | bytes 5013504 | tf_op jit(solution)/shard_map/all_gather | solution.py:310
  15.7 1.6 collective-permute-start.2
  18.3 295.0 %all-gather.15.cloned.1.call-start = ((), (), s32[]{:S(2)}) async-start(), calls=%async_computation.11 | async-start | bytes 5013504 | tf_op jit(solution)/shard_map/all_gather | solution.py:310
  81.4 69.8 %collective-permute-start.1 = (bf16[16,112,768]{2,1,0:T(8,128)(2,1)}, bf16[16,112,768]{2,1,0:T(8,128)(2,1)}, u32[]{:S(2)}, u32[]{:S(2)}) collective-permute-start(bf16[16,112,768]{2,1,0:T(8,128)(2,1)} %bitcast.379), channel_id=1, source_target_pairs={{0,16},{16,0},{1,17},{17,1},{2,18},{18,2},{3,19},{19,3},{4,20},{20... | collective-permute-start | bytes 8257544 | tf_op jit(solution)/shard_map/ppermute | solution.py:202
  81.9 241.5 %copy-start.78 = (f32[512]{0:T(512)}, f32[512]{0:T(512)S(1)}, u32[]{:S(2)}) copy-start(f32[512]{0:T(512)S(1)} %broadcast_multiply_fusion.1) | copy-start | bytes 6148
  82.2 73.4 %copy-start.80 = (f32[512]{0:T(512)}, f32[512]{0:T(512)S(1)}, u32[]{:S(2)}) copy-start(f32[512]{0:T(512)S(1)} %fusion.51) | copy-start | bytes 6148
  148.6 30.7 %collective-permute-start.4 = (bf16[16,112,768]{2,1,0:T(8,128)(2,1)}, bf16[16,112,768]{2,1,0:T(8,128)(2,1)}, u32[]{:S(2)}, u32[]{:S(2)}) collective-permute-start(bf16[16,112,768]{2,1,0:T(8,128)(2,1)} %bitcast.377), channel_id=1, source_target_pairs={{0,16},{16,0},{1,17},{17,1},{2,18},{18,2},{3,19},{19,3},{4,20},{20... | collective-permute-start | bytes 8257544 | tf_op jit(solution)/shard_map/ppermute | solution.py:202
  148.6 174.7 %copy-start.91 = (f32[512]{0:T(512)}, f32[512]{0:T(512)S(1)}, u32[]{:S(2)}) copy-start(f32[512]{0:T(512)S(1)} %fusion.116) | copy-start | bytes 6148
  150.6 532.5 %reduce-scatter.5.cloned.1.call-start = ((), (), s32[]{:S(2)}) async-start(), calls=%async_computation.4 | async-start | bytes 2924544 | tf_op jit(solution)/shard_map/reduce_scatter | solution.py:243
  157.6 165.7 %copy-start.88 = (f32[3072]{0:T(1024)}, f32[3072]{0:T(1024)S(1)}, u32[]{:S(2)}) copy-start(f32[3072]{0:T(1024)S(1)} %reshape.912) | copy-start | bytes 36868
  157.8 15.1 %copy-start.82 = (f32[768]{0:T(1024)}, f32[768]{0:T(1024)S(1)}, u32[]{:S(2)}) copy-start(f32[768]{0:T(1024)S(1)} %reshape.907) | copy-start | bytes 9220
  158.0 165.4 %copy-start.84 = (f32[768]{0:T(1024)}, f32[768]{0:T(1024)S(1)}, u32[]{:S(2)}) copy-start(f32[768]{0:T(1024)S(1)} %reshape.910) | copy-start | bytes 9220
  158.1 165.3 %copy-start.96 = (f32[768]{0:T(1024)}, f32[768]{0:T(1024)S(1)}, u32[]{:S(2)}) copy-start(f32[768]{0:T(1024)S(1)} %reshape.911) | copy-start | bytes 9220
  191.2 170.7 %copy-start.11 = (bf16[16,48,768]{2,1,0:T(8,128)(2,1)}, bf16[16,48,768]{2,1,0:T(8,128)(2,1)S(1)}, u32[]{:S(2)}) copy-start(bf16[16,48,768]{2,1,0:T(8,128)(2,1)S(1)} %get-tuple-element.65) | copy-start | bytes 3538948
  231.0 82.4 %collective-permute-start.3 = (bf16[16,192,768]{2,1,0:T(8,128)(2,1)}, bf16[16,192,768]{2,1,0:T(8,128)(2,1)}, u32[]{:S(2)}, u32[]{:S(2)}) collective-permute-start(bf16[16,192,768]{2,1,0:T(8,128)(2,1)} %bitcast.337), channel_id=1, source_target_pairs={{0,16},{16,0},{1,17},{17,1},{2,18},{18,2},{3,19},{19,3},{4,20},{20... | collective-permute-start | bytes 14155784 | tf_op jit(solution)/shard_map/ppermute | solution.py:202
  313.3 96.3 %collective-permute-start.5 = (bf16[16,192,768]{2,1,0:T(8,128)(2,1)}, bf16[16,192,768]{2,1,0:T(8,128)(2,1)}, u32[]{:S(2)}, u32[]{:S(2)}) collective-permute-start(bf16[16,192,768]{2,1,0:T(8,128)(2,1)} %bitcast.331), channel_id=1, source_target_pairs={{0,16},{16,0},{1,17},{17,1},{2,18},{18,2},{3,19},{19,3},{4,20},{20... | collective-permute-start | bytes 14155784 | tf_op jit(solution)/shard_map/ppermute | solution.py:202
  322.2 19.8 %slice-start.3 = ((s8[4718592]{0:T(1024)(128)(4,1)}), s8[4194304]{0:T(1024)(128)(4,1)S(1)}, s32[]{:S(2)}) async-start(s8[4718592]{0:T(1024)(128)(4,1)} %bitcast.334), calls=%async_computation.15 | async-start | bytes 8388608
  323.3 18.8 %copy-start.13 = (bf16[96,8,4,768]{3,1,2,0:T(8,128)(2,1)}, bf16[96,8,4,768]{3,1,2,0:T(8,128)(2,1)S(1)}, u32[]{:S(2)}) copy-start(bf16[96,8,4,768]{3,1,2,0:T(8,128)(2,1)S(1)} %copy.104) | copy-start | bytes 14155780
  323.6 18.5 %slice-start.4 = ((s8[4718592]{0:T(1024)(128)(4,1)}), s8[524288]{0:T(1024)(128)(4,1)S(1)}, s32[]{:S(2)}) async-start(s8[4718592]{0:T(1024)(128)(4,1)} %bitcast.334), calls=%async_computation.16 | async-start | bytes 1048576
  323.6 18.5 %copy-start.109 = (f32[512,768]{1,0:T(8,128)S(1)}, f32[512,768]{1,0:T(8,128)}, u32[]{:S(2)}) copy-start(f32[512,768]{1,0:T(8,128)} %fusion.182) | copy-start | bytes 4718596
  344.9 209.6 %copy-start.6 = (bf16[512,768]{1,0:T(8,128)(2,1)}, bf16[512,768]{1,0:T(8,128)(2,1)S(1)}, u32[]{:S(2)}) copy-start(bf16[512,768]{1,0:T(8,128)(2,1)S(1)} %get-tuple-element.166) | copy-start | bytes 2359300
  419.7 23.3 %slice-start.5 = ((s8[4718592]{0:T(1024)(128)(4,1)}), s8[4194304]{0:T(1024)(128)(4,1)S(1)}, s32[]{:S(2)}) async-start(s8[4718592]{0:T(1024)(128)(4,1)} %bitcast.339), calls=%async_computation.17 | async-start | bytes 8388608
  421.8 21.2 %slice-start.6 = ((s8[4718592]{0:T(1024)(128)(4,1)}), s8[524288]{0:T(1024)(128)(4,1)S(1)}, s32[]{:S(2)}) async-start(s8[4718592]{0:T(1024)(128)(4,1)} %bitcast.339), calls=%async_computation.18 | async-start | bytes 1048576
  421.9 21.2 %copy-start.65 = (bf16[2,512,768]{2,1,0:T(8,128)(2,1)S(1)}, bf16[2,512,768]{2,1,0:T(8,128)(2,1)}, u32[]{:S(2)}) copy-start(bf16[2,512,768]{2,1,0:T(8,128)(2,1)} %param.17) | copy-start | bytes 4718596
  465.5 48.1 %copy-start.3 = (f32[512,768]{1,0:T(8,128)}, f32[512,768]{1,0:T(8,128)S(1)}, u32[]{:S(2)}) copy-start(f32[512,768]{1,0:T(8,128)S(1)} %get-tuple-element.35) | copy-start | bytes 4718596
  534.3 15.5 %copy-start.14 = (bf16[768,768]{1,0:T(8,128)(2,1)S(1)}, bf16[768,768]{1,0:T(8,128)(2,1)}, u32[]{:S(2)}) copy-start(bf16[768,768]{1,0:T(8,128)(2,1)} %convolution_convert_fusion.4) | copy-start | bytes 3538948
  534.3 15.5 %copy-start.15 = (bf16[768,768]{1,0:T(8,128)(2,1)S(1)}, bf16[768,768]{1,0:T(8,128)(2,1)}, u32[]{:S(2)}) copy-start(bf16[768,768]{1,0:T(8,128)(2,1)} %convolution_convert_fusion.7) | copy-start | bytes 3538948
  534.4 15.5 %copy-start.16 = (bf16[768,768]{1,0:T(8,128)(2,1)S(1)}, bf16[768,768]{1,0:T(8,128)(2,1)}, u32[]{:S(2)}) copy-start(bf16[768,768]{1,0:T(8,128)(2,1)} %convolution_convert_fusion.6) | copy-start | bytes 3538948
  534.4 15.5 %copy-start.17 = (bf16[768,768]{1,0:T(8,128)(2,1)S(1)}, bf16[768,768]{1,0:T(8,128)(2,1)}, u32[]{:S(2)}) copy-start(bf16[768,768]{1,0:T(8,128)(2,1)} %convolution_convert_fusion.5) | copy-start | bytes 3538948
  534.4 15.5 %copy-start.18 = (bf16[768,768]{1,0:T(8,128)(2,1)S(1)}, bf16[768,768]{1,0:T(8,128)(2,1)}, u32[]{:S(2)}) copy-start(bf16[768,768]{1,0:T(8,128)(2,1)} %convolution_convert_fusion.9) | copy-start | bytes 3538948
  534.4 15.5 %copy-start.19 = (bf16[768,768]{1,0:T(8,128)(2,1)S(1)}, bf16[768,768]{1,0:T(8,128)(2,1)}, u32[]{:S(2)}) copy-start(bf16[768,768]{1,0:T(8,128)(2,1)} %convolution_convert_fusion.11) | copy-start | bytes 3538948
  534.4 15.5 %copy-start.20 = (bf16[768,768]{1,0:T(8,128)(2,1)S(1)}, bf16[768,768]{1,0:T(8,128)(2,1)}, u32[]{:S(2)}) copy-start(bf16[768,768]{1,0:T(8,128)(2,1)} %convolution_convert_fusion.10) | copy-start | bytes 3538948
  540.6 5.3 collective-permute-start.8
  541.1 8.7 collective-permute-start.9
  554.4 263.2 %reduce-scatter.7.cloned.1.call-start = ((), (), s32[]{:S(2)}) async-start(), calls=%async_computation.5 | async-start | bytes 2924544 | tf_op jit(solution)/shard_map/reduce_scatter | solution.py:243
  581.9 8.3 collective-permute-start.12
  582.3 377.2 %reduce-scatter.11.cloned.1.call-start = ((), (), s32[]{:S(2)}) async-start(), calls=%async_computation.7 | async-start | bytes 5013504 | tf_op jit(solution)/shard_map/reduce_scatter | solution.py:243
  598.5 503.7 %reduce-scatter.9.cloned.1.call-start = ((), (), s32[]{:S(2)}) async-start(), calls=%async_computation.6 | async-start | bytes 5013504 | tf_op jit(solution)/shard_map/reduce_scatter | solution.py:243
  623.9 9.6 collective-permute-start.11
  645.1 6.0 collective-permute-start.7
  645.8 3.9 collective-permute-start.6
  818.6 2.0 collective-permute-start.10
  1103.3 1.6 collective-permute-start.13
  (95 other events, 379.8 us)
Sparse Core Ops, SparseCore 0:
  13.9 67.4 all-gather.8
  84.7 63.8 all-gather.12
  151.4 79.4 all-gather.10
  234.2 79.0 all-gather.14
  554.6 128.4 reduce-scatter.4
  688.7 128.9 reduce-scatter.6
  822.9 136.6 reduce-scatter.10
  965.5 136.6 reduce-scatter.8

commit v2 on v1

--- a/solution.py
+++ b/solution.py
@@ -202,6 +202,60 @@
     return lax.ppermute(value, "section", [(0, 1), (1, 0)])
 
 
+def link_orders(count):
+    bits = list(range(count.bit_length() - 1))
+    near, far = bits[:3], bits[3:]
+    return [near[turn:] + near[:turn] + far for turn in range(max(1, len(near)))]
+
+
+def row_parts(height, parts):
+    step = 8 * -(-height // (8 * parts))
+    edges = [min(height, step * part) for part in range(parts + 1)]
+    return [(low, high) for low, high in zip(edges, edges[1:]) if high > low]
+
+
+def exchange(value, bit, count):
+    return lax.ppermute(value, "dp", [(source, source ^ (1 << bit)) for source in range(count)])
+
+
+def gather_dp(piece, count):
+    orders = link_orders(count)
+    places = count.bit_length() - 1
+    me = lax.axis_index("dp")
+    done = []
+    for (low, high), order in zip(row_parts(piece.shape[0], len(orders)), orders):
+        held = piece[low:high].reshape((1,) * places + (high - low, piece.shape[1]))
+        for bit in reversed(order):
+            other = exchange(held, bit, count)
+            axis = places - 1 - bit
+            mine = (me >> bit) & 1
+            held = jnp.where(
+                mine == 0,
+                jnp.concatenate([held, other], axis=axis),
+                jnp.concatenate([other, held], axis=axis),
+            )
+        done.append(held.reshape(count, high - low, piece.shape[1]))
+    return jnp.concatenate(done, axis=1)
+
+
+def scatter_sum_dp(whole, count):
+    orders = link_orders(count)
+    places = count.bit_length() - 1
+    me = lax.axis_index("dp")
+    done = []
+    for (low, high), order in zip(row_parts(whole.shape[1], len(orders)), orders):
+        held = whole[:, low:high].reshape((2,) * places + (high - low, whole.shape[2]))
+        for bit in order:
+            axis = places - 1 - bit
+            mine = (me >> bit) & 1
+            sent = lax.dynamic_index_in_dim(held, 1 - mine, axis, keepdims=True)
+            kept = lax.dynamic_index_in_dim(held, mine, axis, keepdims=True)
+            arrived = exchange(sent, bit, count)
+            held = (kept.astype(jnp.float32) + arrived.astype(jnp.float32)).astype(jnp.bfloat16)
+        done.append(held.reshape(high - low, whole.shape[2]))
+    return jnp.concatenate(done, axis=0)
+
+
 def column_blocks(shard, width):
     return jnp.concatenate(jnp.split(shard, shard.shape[1] // width, axis=1), axis=0)
 
@@ -240,7 +294,7 @@
     arrived = swap(jnp.where(core == 0, high, low))
     own = jnp.where(core == 0, low, high)
     total = (own.astype(jnp.float32) + arrived.astype(jnp.float32)).astype(jnp.bfloat16)
-    return lax.psum_scatter(total, "dp", scatter_dimension=0, tiled=False)
+    return scatter_sum_dp(total, total.shape[0])
 
 
 def reduce_mlp(grads, core, count, width):
@@ -307,7 +361,7 @@
         own = jnp.where(core == 0, low, high)
         pieces.append((jnp.where(core == 0, own, arrived), jnp.where(core == 0, arrived, own)))
     gathered = [
-        tuple(lax.all_gather(piece[layer], "dp", axis=0, tiled=False) for piece in pieces)
+        tuple(gather_dp(piece[layer], count) for piece in pieces)
         for layer in range(2)
     ]
     parameters = [unpack(gathered[layer], core, width, units) for layer in range(2)]

time: 1120 us -> 755 us (0.67)
  waiting for transfers between devices: 703 us -> 194 us
  starting transfers between devices: 5.57 us -> 131 us
  other arithmetic: 97.8 us -> 113 us
  local copies, waits for them, and re-layouts: 94.4 us -> 107 us
  between operations: 16.1 us -> 4.37 us
    reduce_scatter x4 -> x0, waiting for transfers between devices: 445 us -> none  [reduce_pair(): return lax.psum_scatter(total, 'dp', scatter_dimension=0, tiled=False)]
    all_gather x4 -> x0, waiting for transfers between devices: 227 us -> none  [on_device(): lax.all_gather(piece[layer], 'dp', axis=0, tiled=False)]
    ppermute x0 -> x96, waiting for transfers between devices: none -> 193 us  [exchange(): lax.ppermute(value, 'dp', [(source, source ^ 1 << bit) for source in rang...]
    ppermute x0 -> x96, starting transfers between devices: none -> 128 us  [exchange(): lax.ppermute(value, 'dp', [(source, source ^ 1 << bit) for source in rang...]
    ppermute x14, waiting for transfers between devices: 30.6 us -> 0.81 us  [swap(): return lax.ppermute(value, 'section', [(0, 1), (1, 0)])]
    reshape x2 -> x3, local copies, waits for them, and re-layouts: 19.5 us -> 23.1 us  [reduce_mlp(): up = grads[2].astype(jnp.bfloat16).reshape(count, rows, -1, width)]
  transfers between devices with their start and end apart: 22 -> 110, of which waited for: 16 -> 49; matrix products, arithmetic and copies ran while one was open for 21% -> 38% of each run, Pallas kernels for 0% -> 0%
where the time goes in v2:
time: 755 us; the launch traced here: 745 us
  matrix products  196 us (26%)
  waiting for transfers between devices  194 us (26%)
  starting transfers between devices  131 us (17%)
  other arithmetic  113 us (15%)
  local copies, waits for them, and re-layouts  107 us (14%)
    ppermute x96, waiting for transfers between devices, exchange(): lax.ppermute(value, 'dp', [(source, source ^ 1 << bit) for source in rang...  193 us
    ppermute x96, starting transfers between devices, exchange(): lax.ppermute(value, 'dp', [(source, source ^ 1 << bit) for source in rang...  128 us
    dot_general x2, matrix products, layer_forward(): jnp.dot(normed_m, up_w, preferred_element_type=jnp.float32)  39.6 us
    reshape x3, local copies, waits for them, and re-layouts, reduce_mlp(): up = grads[2].astype(jnp.bfloat16).reshape(count, rows, -1, width)  23.1 us
    dot_general x6, matrix products, layer_forward(): jnp.dot(normed_a, part, preferred_element_type=jnp.float32)  17.8 us
    dot_general x2, matrix products, layer_backward(): jnp.einsum('td,fd->tf', up_low, down_w, preferred_element_type=jnp.float32)  17.3 us
    convert_element_type x3, other arithmetic, reduce_pair(): (own.astype(jnp.float32) + arrived.astype(jnp.float32)).astype(jnp.bfloat16)  15.6 us
  transfers between devices with their start and end apart: 110, of which 49 were waited for; matrix products, arithmetic and copies ran while one was open for 38% of the time, Pallas kernels for 0%

profile of v2, /device:TPU:0, one launch (start us, length us, event | category | flops | bytes accessed | tf_op | source)
XLA Modules:
  0.0 744.8 jit_solution(4082587552051226604)
XLA Ops:
  11.4 4.1 collective-permute-start.9
  24.1 4.1 collective-permute-done.1
  48.2 11.2 %collective-permute-done.49 = bf16[1,1,1,1,64,768]{5,4,3,2,1,0:T(8,128)(2,1)S(1)} collective-permute-done((bf16[1,1,1,1,64,768]{5,4,3,2,1,0:T(8,128)(2,1)S(1)}, bf16[1,1,1,1,64,768]{5,4,3,2,1,0:T(8,128)(2,1)S(1)}, u32[]{:S(2)}, u32[]{:S(2)}) %collective-permute-start.49) | collective-permute-done | bytes 98336 | tf_op jit(solution)/shard_map/ppermute | solution.py:218
  61.7 5.0 collective-permute-done.23
  78.6 4.9 collective-permute-done.42
  103.5 7.3 collective-permute-done.39
  115.0 8.2 %collective-permute-done.4 = bf16[2,2,2,1,40,768]{5,4,3,2,1,0:T(8,128)(2,1)S(1)} collective-permute-done((bf16[2,2,2,1,40,768]{5,4,3,2,1,0:T(8,128)(2,1)S(1)}, bf16[2,2,2,1,40,768]{5,4,3,2,1,0:T(8,128)(2,1)S(1)}, u32[]{:S(2)}, u32[]{:S(2)}) %collective-permute-start.4) | collective-permute-done | bytes 491552 | tf_op jit(solution)/shard_map/ppermute | solution.py:218
  126.6 4.4 collective-permute-done.25
  135.5 9.7 %collective-permute-done.31 = bf16[2,2,2,1,40,768]{5,4,3,2,1,0:T(8,128)(2,1)S(1)} collective-permute-done((bf16[2,2,2,1,40,768]{5,4,3,2,1,0:T(8,128)(2,1)S(1)}, bf16[2,2,2,1,40,768]{5,4,3,2,1,0:T(8,128)(2,1)S(1)}, u32[]{:S(2)}, u32[]{:S(2)}) %collective-permute-start.31) | collective-permute-done | bytes 491552 | tf_op jit(solution)/shard_map/ppermute | solution.py:218
  146.9 5.5 collective-permute-done.26
  152.7 9.0 %collective-permute-done.18 = bf16[2,2,2,1,64,768]{5,4,3,2,1,0:T(8,128)(2,1)S(1)} collective-permute-done((bf16[2,2,2,1,64,768]{5,4,3,2,1,0:T(8,128)(2,1)S(1)}, bf16[2,2,2,1,64,768]{5,4,3,2,1,0:T(8,128)(2,1)S(1)}, u32[]{:S(2)}, u32[]{:S(2)}) %collective-permute-start.18) | collective-permute-done | bytes 786464 | tf_op jit(solution)/shard_map/ppermute | solution.py:218
  170.2 10.7 %collective-permute-done.52 = bf16[2,1,2,2,64,768]{5,4,3,2,1,0:T(8,128)(2,1)S(1)} collective-permute-done((bf16[2,1,2,2,64,768]{5,4,3,2,1,0:T(8,128)(2,1)S(1)}, bf16[2,1,2,2,64,768]{5,4,3,2,1,0:T(8,128)(2,1)S(1)}, u32[]{:S(2)}, u32[]{:S(2)}) %collective-permute-start.52) | collective-permute-done | bytes 786464 | tf_op jit(solution)/shard_map/ppermute | solution.py:218
  250.0 4.0 fusion.81
  256.0 4.4 broadcast_select_fusion.2
  264.3 18.4 %multiply_convert_fusion.3 = (bf16[512,3072]{1,0:T(8,128)(2,1)S(1)}, f32[512,3072]{1,0:T(8,128)}, f32[512,3072]{1,0:T(8,128)}) fusion(f32[3072]{0:T(1024)S(1)} %copy-done.105, bf16[768,3072]{1,0:T(8,128)(2,1)S(1)} %bitcast.565, f32[768]{0:T(1024)S(1)} %reshape.6747, f32[768]{0:T(1024)S(1)} %reshape.6746, f32[512]{0:T(512)S(1)} %copy-done.108, ...), kind=kOutput, calls=%fused_computation.41 | convolution fusion | flops 2522087424 | bytes 21258244 | tf_op jit(solution)/shard_map/dot_general | solution.py:86
  309.5 7.1 multiply_reduce_fusion.1
  316.6 7.0 multiply_convert_fusion.1
  328.7 4.0 fusion.80
  348.2 4.6 broadcast_select_fusion
  358.5 21.2 %multiply_convert_fusion.2 = (bf16[512,3072]{1,0:T(8,128)(2,1)}, f32[512,3072]{1,0:T(8,128)}, f32[512,3072]{1,0:T(8,128)}) fusion(f32[3072]{0:T(1024)S(1)} %copy-done.107, bf16[768,3072]{1,0:T(8,128)(2,1)S(1)} %bitcast.567, bf16[512,768]{1,0:T(8,128)(2,1)S(1)} %get-tuple-element.230, f32[768]{0:T(1024)S(1)} %copy-done.116, f32[768]{0:T(1024)S(1)} %copy-done.91, ...), kind=kOutput, calls=%fused_computation.28 | convolution fusion | flops 2522087424 | bytes 21256192 | tf_op jit(solution)/shard_map/dot_general | solution.py:86
  379.7 7.7 %fusion.229 = (bf16[3072]{0:T(1024)(128)(2,1)S(1)}, bf16[512,3072]{1,0:T(8,128)(2,1)S(1)}) fusion(f32[512,3072]{1,0:T(8,128)} %get-tuple-element.53, bf16[3072,768]{1,0:T(8,128)(2,1)S(1)} %bitcast.571, bf16[2,512,768]{2,1,0:T(8,128)(2,1)S(1)} %copy-done.82, s32[]{:T(128)S(6)} %select_n.1520, f32[512,3072]{1,0:T(8,128)} %get-tuple-element.231, ...), kind=kOutput, calls=%fused_computation.642 | convolution fusion | flops 2441081856 | bytes 21252100 | tf_op jit(solution)/shard_map/td,fd->tf/dot_general | solution.py:136
  394.9 4.6 convert_reduce_fusion.2
  405.3 8.1 %bitcast_reduce_fusion = (bf16[12,64]{1,0:T(8,128)(2,1)S(1)}, bf16[12,64,512]{2,1,0:T(8,128)(2,1)S(1)}) fusion(bf16[512,12,64]{0,2,1:T(8,128)(2,1)} %bitcast.613, f32[12,512]{1,0:T(8,128)S(1)} %copy-done.90, f32[12,512,512]{1,2,0:T(8,128)} %copy-done, pred[512,512]{0,1:T(8,128)(4,1)S(1)} %compare_and_fusion), kind=kOutput, calls=%fused_computation.227 | convolution fusion | flops 416021760 | bytes 14444032 | tf_op jit(solution)/shard_map/hts,thd->shd/dot_general | solution.py:148
  417.7 4.8 convolution_convert_fusion.1
  422.5 4.4 convolution_convert_fusion
  427.2 6.8 multiply_reduce_fusion
  434.0 7.4 multiply_convert_fusion
  455.4 9.6 %fusion.228 = (bf16[3072]{0:T(1024)(128)(2,1)S(1)}, bf16[512,3072]{1,0:T(8,128)(2,1)}) fusion(f32[512,3072]{1,0:T(8,128)} %get-tuple-element.55, bf16[3072,768]{1,0:T(8,128)(2,1)} %bitcast.570, f32[512,768]{1,0:T(8,128)S(1)} %get-tuple-element.35, f32[512,3072]{1,0:T(8,128)} %get-tuple-element.228, f32[3072]{0:T(1024)S(1)} %copy-done.106), kind=kOutput, calls=%fused_computation.641 | convolution fusion | flops 2441475072 | bytes 22038528 | tf_op jit(solution)/shard_map/td,fd->tf/dot_general | solution.py:136
  466.0 9.9 %reshape.6733 = bf16[16,48,4,768]{3,2,1,0:T(4,128)(2,1)} reshape(bf16[768,3072]{1,0:T(8,128)(2,1)} %convolution_convert_fusion.1) | data formatting | bytes 9437184 | tf_op jit(solution)/shard_map/reshape | solution.py:302
  475.9 5.3 copy.219
  481.6 9.6 %fusion.48 = (bf16[768]{0:T(1024)(128)(2,1)S(1)}, f32[512]{0:T(512)S(1)}, f32[512]{0:T(512)S(1)}, bf16[768]{0:T(1024)(128)(2,1)S(1)}, bf16[768]{0:T(1024)(128)(2...) fusion(f32[512]{0:T(512)S(1)} %copy-done.109, f32[512]{0:T(512)S(1)} %copy-done.96, ...), kind=kOutput, calls=%fused_computation.121 | convolution fusion | flops 2422599680 | bytes 16535556 | tf_op jit(solution)/shard_map/tf,df->td/dot_general | solution.py:141
  491.3 4.6 fusion.213
  501.0 6.4 broadcast_select_fusion.5
  511.5 4.4 convolution_convert_fusion.2
  515.9 4.8 convolution_convert_fusion.3
  520.7 9.8 %reshape.6724 = bf16[16,48,4,768]{3,2,1,0:T(4,128)(2,1)} reshape(bf16[768,3072]{1,0:T(8,128)(2,1)} %convolution_convert_fusion.3) | data formatting | bytes 9437184 | tf_op jit(solution)/shard_map/reshape | solution.py:302
  546.1 5.1 add_convert_fusion.5
  555.5 8.2 %collective-permute-done.65 = bf16[2,1,2,2,32,768]{5,4,3,2,1,0:T(8,128)(2,1)S(1)} collective-permute-done((bf16[2,1,2,2,32,768]{5,4,3,2,1,0:T(8,128)(2,1)S(1)}, bf16[2,1,2,2,32,768]{5,4,3,2,1,0:T(8,128)(2,1)S(1)}, u32[]{:S(2)}, u32[]{:S(2)}) %collective-permute-start.65) | collective-permute-done | bytes 393248 | tf_op jit(solution)/shard_map/ppermute | solution.py:218
  565.3 6.2 collective-permute-done.78
  578.5 7.1 collective-permute-done.70
  598.5 4.1 collective-permute-done.80
  637.5 6.0 add_convert_fusion
  650.7 4.5 add_convert_fusion.1
  658.0 7.0 collective-permute-done.101
  672.9 8.8 %collective-permute-done.88 = bf16[2,2,1,2,64,768]{5,4,3,2,1,0:T(8,128)(2,1)S(1)} collective-permute-done((bf16[2,2,1,2,64,768]{5,4,3,2,1,0:T(8,128)(2,1)S(1)}, bf16[2,2,1,2,64,768]{5,4,3,2,1,0:T(8,128)(2,1)S(1)}, u32[]{:S(2)}, u32[]{:S(2)}) %collective-permute-start.88) | collective-permute-done | bytes 786464 | tf_op jit(solution)/shard_map/ppermute | solution.py:218
  687.3 6.6 collective-permute-done.102
  719.6 9.1 %collective-permute-done.104 = bf16[1,1,1,1,64,768]{5,4,3,2,1,0:T(8,128)(2,1)S(1)} collective-permute-done((bf16[1,1,1,1,64,768]{5,4,3,2,1,0:T(8,128)(2,1)S(1)}, bf16[1,1,1,1,64,768]{5,4,3,2,1,0:T(8,128)(2,1)S(1)}, u32[]{:S(2)}, u32[]{:S(2)}) %collective-permute-start.104) | collective-permute-done | bytes 98336 | tf_op jit(solution)/shard_map/ppermute | solution.py:218
  730.8 4.2 collective-permute-done.108
  (866 shorter events, 400.6 us)
Async XLA Ops:
  6.2 30.6 %collective-permute-start.14 = (bf16[192,768]{1,0:T(8,128)(2,1)}, bf16[192,768]{1,0:T(8,128)(2,1)}, u32[]{:S(2)}, u32[]{:S(2)}) collective-permute-start(bf16[192,768]{1,0:T(8,128)(2,1)} %bitcast_select_fusion.4), channel_id=1, source_target_pairs={{0,16},{16,0},{1,17},{17,1},{2,18},{18,2},{3,19},{19,3},{4,20},{20... | collective-permute-start | bytes 884744 | tf_op jit(solution)/shard_map/ppermute | solution.py:202
  15.6 18.0 %collective-permute-start.28 = (bf16[1,1,1,1,40,768]{5,4,3,2,1,0:T(8,128)(2,1)S(1)}, bf16[1,1,1,1,40,768]{5,4,3,2,1,0:T(8,128)(2,1)S(1)}, u32[]{:S(2)}, u32[]{:S(2)}) collective-permute-start(bf16[1,1,1,1,40,768]{5,4,3,2,1,0:T(8,128)(2,1)S(1)} %get-tuple-element.168), channel_id=1, source_target_pairs={{0,8},{1,9},{2,10},{3,11},{4,12},{5,13},{6,14},{7,15},{8,0},{9,1},... | collective-permute-start | bytes 184328 | tf_op jit(solution)/shard_map/ppermute | solution.py:218
  38.8 20.6 %collective-permute-start.41 = (bf16[1,1,1,1,64,768]{5,4,3,2,1,0:T(8,128)(2,1)S(1)}, bf16[1,1,1,1,64,768]{5,4,3,2,1,0:T(8,128)(2,1)S(1)}, u32[]{:S(2)}, u32[]{:S(2)}) collective-permute-start(bf16[1,1,1,1,64,768]{5,4,3,2,1,0:T(8,128)(2,1)S(1)} %get-tuple-element.134), channel_id=1, source_target_pairs={{0,8},{1,9},{2,10},{3,11},{4,12},{5,13},{6,14},{7,15},{8,0},{9,1},... | collective-permute-start | bytes 294920 | tf_op jit(solution)/shard_map/ppermute | solution.py:218
  41.8 19.3 %collective-permute-start.45 = (bf16[1,1,1,1,64,768]{5,4,3,2,1,0:T(8,128)(2,1)S(1)}, bf16[1,1,1,1,64,768]{5,4,3,2,1,0:T(8,128)(2,1)S(1)}, u32[]{:S(2)}, u32[]{:S(2)}) collective-permute-start(bf16[1,1,1,1,64,768]{5,4,3,2,1,0:T(8,128)(2,1)S(1)} %get-tuple-element.135), channel_id=1, source_target_pairs={{0,8},{1,9},{2,10},{3,11},{4,12},{5,13},{6,14},{7,15},{8,0},{9,1},... | collective-permute-start | bytes 294920 | tf_op jit(solution)/shard_map/ppermute | solution.py:218
  44.9 22.5 %collective-permute-start.15 = (bf16[1,1,1,1,64,768]{5,4,3,2,1,0:T(8,128)(2,1)S(1)}, bf16[1,1,1,1,64,768]{5,4,3,2,1,0:T(8,128)(2,1)S(1)}, u32[]{:S(2)}, u32[]{:S(2)}) collective-permute-start(bf16[1,1,1,1,64,768]{5,4,3,2,1,0:T(8,128)(2,1)S(1)} %get-tuple-element.140), channel_id=1, source_target_pairs={{0,8},{1,9},{2,10},{3,11},{4,12},{5,13},{6,14},{7,15},{8,0},{9,1},... | collective-permute-start | bytes 294920 | tf_op jit(solution)/shard_map/ppermute | solution.py:218
  46.7 21.0 %collective-permute-start.19 = (bf16[1,1,1,1,64,768]{5,4,3,2,1,0:T(8,128)(2,1)S(1)}, bf16[1,1,1,1,64,768]{5,4,3,2,1,0:T(8,128)(2,1)S(1)}, u32[]{:S(2)}, u32[]{:S(2)}) collective-permute-start(bf16[1,1,1,1,64,768]{5,4,3,2,1,0:T(8,128)(2,1)S(1)} %get-tuple-element.141), channel_id=1, source_target_pairs={{0,8},{1,9},{2,10},{3,11},{4,12},{5,13},{6,14},{7,15},{8,0},{9,1},... | collective-permute-start | bytes 294920 | tf_op jit(solution)/shard_map/ppermute | solution.py:218
  66.7 25.2 %collective-permute-start.30 = (bf16[2,2,1,1,40,768]{5,4,3,2,1,0:T(8,128)(2,1)S(1)}, bf16[2,2,1,1,40,768]{5,4,3,2,1,0:T(8,128)(2,1)S(1)}, u32[]{:S(2)}, u32[]{:S(2)}) collective-permute-start(bf16[2,2,1,1,40,768]{5,4,3,2,1,0:T(8,128)(2,1)S(1)} %maximum_select_fusion.41), channel_id=1, source_target_pairs={{0,2},{1,3},{2,0},{3,1},{4,6},{5,7},{6,4},{7,5},{8,10},{9,11},{10,... | collective-permute-start | bytes 737288 | tf_op jit(solution)/shard_map/ppermute | solution.py:218
  67.4 26.2 %collective-permute-start.7 = (bf16[2,1,1,2,40,768]{5,4,3,2,1,0:T(8,128)(2,1)S(1)}, bf16[2,1,1,2,40,768]{5,4,3,2,1,0:T(8,128)(2,1)S(1)}, u32[]{:S(2)}, u32[]{:S(2)}) collective-permute-start(bf16[2,1,1,2,40,768]{5,4,3,2,1,0:T(8,128)(2,1)S(1)} %maximum_select_fusion.39), channel_id=1, source_target_pairs={{0,4},{1,5},{2,6},{3,7},{4,0},{5,1},{6,2},{7,3},{8,12},{9,13},{10,... | collective-permute-start | bytes 737288 | tf_op jit(solution)/shard_map/ppermute | solution.py:218
  67.7 26.6 %collective-permute-start.34 = (bf16[2,1,1,2,40,768]{5,4,3,2,1,0:T(8,128)(2,1)S(1)}, bf16[2,1,1,2,40,768]{5,4,3,2,1,0:T(8,128)(2,1)S(1)}, u32[]{:S(2)}, u32[]{:S(2)}) collective-permute-start(bf16[2,1,1,2,40,768]{5,4,3,2,1,0:T(8,128)(2,1)S(1)} %maximum_select_fusion.43), channel_id=1, source_target_pairs={{0,4},{1,5},{2,6},{3,7},{4,0},{5,1},{6,2},{7,3},{8,12},{9,13},{10,... | collective-permute-start | bytes 737288 | tf_op jit(solution)/shard_map/ppermute | solution.py:218
  91.9 18.9 %collective-permute-start.39 = (bf16[2,1,2,2,32,768]{5,4,3,2,1,0:T(8,128)(2,1)S(1)}, bf16[2,1,2,2,32,768]{5,4,3,2,1,0:T(8,128)(2,1)S(1)}, u32[]{:S(2)}, u32[]{:S(2)}) collective-permute-start(bf16[2,1,2,2,32,768]{5,4,3,2,1,0:T(8,128)(2,1)S(1)} %maximum_select_fusion.29), channel_id=1, source_target_pairs={{0,4},{1,5},{2,6},{3,7},{4,0},{5,1},{6,2},{7,3},{8,12},{9,13},{10,... | collective-permute-start | bytes 1179656 | tf_op jit(solution)/shard_map/ppermute | solution.py:218
  93.6 19.8 %collective-permute-start.43 = (bf16[2,2,1,1,64,768]{5,4,3,2,1,0:T(8,128)(2,1)S(1)}, bf16[2,2,1,1,64,768]{5,4,3,2,1,0:T(8,128)(2,1)S(1)}, u32[]{:S(2)}, u32[]{:S(2)}) collective-permute-start(bf16[2,2,1,1,64,768]{5,4,3,2,1,0:T(8,128)(2,1)S(1)} %maximum_select_fusion.31), channel_id=1, source_target_pairs={{0,2},{1,3},{2,0},{3,1},{4,6},{5,7},{6,4},{7,5},{8,10},{9,11},{10,... | collective-permute-start | bytes 1179656 | tf_op jit(solution)/shard_map/ppermute | solution.py:218
  94.3 18.1 %collective-permute-start.17 = (bf16[2,2,1,1,64,768]{5,4,3,2,1,0:T(8,128)(2,1)S(1)}, bf16[2,2,1,1,64,768]{5,4,3,2,1,0:T(8,128)(2,1)S(1)}, u32[]{:S(2)}, u32[]{:S(2)}) collective-permute-start(bf16[2,2,1,1,64,768]{5,4,3,2,1,0:T(8,128)(2,1)S(1)} %maximum_select_fusion.24), channel_id=1, source_target_pairs={{0,2},{1,3},{2,0},{3,1},{4,6},{5,7},{6,4},{7,5},{8,10},{9,11},{10,... | collective-permute-start | bytes 1179656 | tf_op jit(solution)/shard_map/ppermute | solution.py:218
  98.0 33.1 %collective-permute-start.51 = (bf16[2,1,2,1,64,768]{5,4,3,2,1,0:T(8,128)(2,1)S(1)}, bf16[2,1,2,1,64,768]{5,4,3,2,1,0:T(8,128)(2,1)S(1)}, u32[]{:S(2)}, u32[]{:S(2)}) collective-permute-start(bf16[2,1,2,1,64,768]{5,4,3,2,1,0:T(8,128)(2,1)S(1)} %maximum_select_fusion.35), channel_id=1, source_target_pairs={{0,1},{1,0},{2,3},{3,2},{4,5},{5,4},{6,7},{7,6},{8,9},{9,8},{10,11... | collective-permute-start | bytes 1179656 | tf_op jit(solution)/shard_map/ppermute | solution.py:218
  103.0 29.7 %collective-permute-start.47 = (bf16[2,1,1,2,64,768]{5,4,3,2,1,0:T(8,128)(2,1)S(1)}, bf16[2,1,1,2,64,768]{5,4,3,2,1,0:T(8,128)(2,1)S(1)}, u32[]{:S(2)}, u32[]{:S(2)}) collective-permute-start(bf16[2,1,1,2,64,768]{5,4,3,2,1,0:T(8,128)(2,1)S(1)} %maximum_select_fusion.33), channel_id=1, source_target_pairs={{0,4},{1,5},{2,6},{3,7},{4,0},{5,1},{6,2},{7,3},{8,12},{9,13},{10,... | collective-permute-start | bytes 1179656 | tf_op jit(solution)/shard_map/ppermute | solution.py:218
  113.4 19.7 %collective-permute-start.21 = (bf16[2,1,1,2,64,768]{5,4,3,2,1,0:T(8,128)(2,1)S(1)}, bf16[2,1,1,2,64,768]{5,4,3,2,1,0:T(8,128)(2,1)S(1)}, u32[]{:S(2)}, u32[]{:S(2)}) collective-permute-start(bf16[2,1,1,2,64,768]{5,4,3,2,1,0:T(8,128)(2,1)S(1)} %maximum_select_fusion.26), channel_id=1, source_target_pairs={{0,4},{1,5},{2,6},{3,7},{4,0},{5,1},{6,2},{7,3},{8,12},{9,13},{10,... | collective-permute-start | bytes 1179656 | tf_op jit(solution)/shard_map/ppermute | solution.py:218
  131.0 53.6 %collective-permute-start.13 = (bf16[16,112,768]{2,1,0:T(8,128)(2,1)S(1)}, bf16[16,112,768]{2,1,0:T(8,128)(2,1)S(1)}, u32[]{:S(2)}, u32[]{:S(2)}) collective-permute-start(bf16[16,112,768]{2,1,0:T(8,128)(2,1)S(1)} %pad_maximum_fusion.2), channel_id=1, source_target_pairs={{0,16},{16,0},{1,17},{17,1},{2,18},{18,2},{3,19},{19,3},{4,20},{20... | collective-permute-start | bytes 8257544 | tf_op jit(solution)/shard_map/ppermute | solution.py:202
  132.7 19.7 %collective-permute-start.26 = (bf16[2,1,2,2,64,768]{5,4,3,2,1,0:T(8,128)(2,1)S(1)}, bf16[2,1,2,2,64,768]{5,4,3,2,1,0:T(8,128)(2,1)S(1)}, u32[]{:S(2)}, u32[]{:S(2)}) collective-permute-start(bf16[2,1,2,2,64,768]{5,4,3,2,1,0:T(8,128)(2,1)S(1)} %maximum_select_fusion.13), channel_id=1, source_target_pairs={{0,4},{1,5},{2,6},{3,7},{4,0},{5,1},{6,2},{7,3},{8,12},{9,13},{10,... | collective-permute-start | bytes 2359304 | tf_op jit(solution)/shard_map/ppermute | solution.py:218
  133.1 28.6 %collective-permute-start.18 = (bf16[2,2,2,1,64,768]{5,4,3,2,1,0:T(8,128)(2,1)S(1)}, bf16[2,2,2,1,64,768]{5,4,3,2,1,0:T(8,128)(2,1)S(1)}, u32[]{:S(2)}, u32[]{:S(2)}) collective-permute-start(bf16[2,2,2,1,64,768]{5,4,3,2,1,0:T(8,128)(2,1)S(1)} %maximum_select_fusion.11), channel_id=1, source_target_pairs={{0,1},{1,0},{2,3},{3,2},{4,5},{5,4},{6,7},{7,6},{8,9},{9,8},{10,11... | collective-permute-start | bytes 2359304 | tf_op jit(solution)/shard_map/ppermute | solution.py:218
  133.9 28.2 %collective-permute-start.22 = (bf16[2,2,1,2,64,768]{5,4,3,2,1,0:T(8,128)(2,1)S(1)}, bf16[2,2,1,2,64,768]{5,4,3,2,1,0:T(8,128)(2,1)S(1)}, u32[]{:S(2)}, u32[]{:S(2)}) collective-permute-start(bf16[2,2,1,2,64,768]{5,4,3,2,1,0:T(8,128)(2,1)S(1)} %maximum_select_fusion.12), channel_id=1, source_target_pairs={{0,2},{1,3},{2,0},{3,1},{4,6},{5,7},{6,4},{7,5},{8,10},{9,11},{10,... | collective-permute-start | bytes 2359304 | tf_op jit(solution)/shard_map/ppermute | solution.py:218
  145.2 24.8 %collective-permute-start.48 = (bf16[2,2,1,2,64,768]{5,4,3,2,1,0:T(8,128)(2,1)S(1)}, bf16[2,2,1,2,64,768]{5,4,3,2,1,0:T(8,128)(2,1)S(1)}, u32[]{:S(2)}, u32[]{:S(2)}) collective-permute-start(bf16[2,2,1,2,64,768]{5,4,3,2,1,0:T(8,128)(2,1)S(1)} %maximum_select_fusion.16), channel_id=1, source_target_pairs={{0,2},{1,3},{2,0},{3,1},{4,6},{5,7},{6,4},{7,5},{8,10},{9,11},{10,... | collective-permute-start | bytes 2359304 | tf_op jit(solution)/shard_map/ppermute | solution.py:218
  152.4 36.4 %collective-permute-start.40 = (bf16[16,112,768]{2,1,0:T(8,128)(2,1)S(1)}, bf16[16,112,768]{2,1,0:T(8,128)(2,1)S(1)}, u32[]{:S(2)}, u32[]{:S(2)}) collective-permute-start(bf16[16,112,768]{2,1,0:T(8,128)(2,1)S(1)} %pad_maximum_fusion.3), channel_id=1, source_target_pairs={{0,16},{16,0},{1,17},{17,1},{2,18},{18,2},{3,19},{19,3},{4,20},{20... | collective-permute-start | bytes 8257544 | tf_op jit(solution)/shard_map/ppermute | solution.py:202
  161.7 19.2 %collective-permute-start.52 = (bf16[2,1,2,2,64,768]{5,4,3,2,1,0:T(8,128)(2,1)S(1)}, bf16[2,1,2,2,64,768]{5,4,3,2,1,0:T(8,128)(2,1)S(1)}, u32[]{:S(2)}, u32[]{:S(2)}) collective-permute-start(bf16[2,1,2,2,64,768]{5,4,3,2,1,0:T(8,128)(2,1)S(1)} %maximum_select_fusion.17), channel_id=1, source_target_pairs={{0,4},{1,5},{2,6},{3,7},{4,0},{5,1},{6,2},{7,3},{8,12},{9,13},{10,... | collective-permute-start | bytes 2359304 | tf_op jit(solution)/shard_map/ppermute | solution.py:218
  162.1 19.0 %collective-permute-start.44 = (bf16[2,2,2,1,64,768]{5,4,3,2,1,0:T(8,128)(2,1)S(1)}, bf16[2,2,2,1,64,768]{5,4,3,2,1,0:T(8,128)(2,1)S(1)}, u32[]{:S(2)}, u32[]{:S(2)}) collective-permute-start(bf16[2,2,2,1,64,768]{5,4,3,2,1,0:T(8,128)(2,1)S(1)} %maximum_select_fusion.15), channel_id=1, source_target_pairs={{0,1},{1,0},{2,3},{3,2},{4,5},{5,4},{6,7},{7,6},{8,9},{9,8},{10,11... | collective-permute-start | bytes 2359304 | tf_op jit(solution)/shard_map/ppermute | solution.py:218
  170.0 86.1 %collective-permute-start.27 = (bf16[16,192,768]{2,1,0:T(8,128)(2,1)}, bf16[16,192,768]{2,1,0:T(8,128)(2,1)}, u32[]{:S(2)}, u32[]{:S(2)}) collective-permute-start(bf16[16,192,768]{2,1,0:T(8,128)(2,1)} %pad_maximum_fusion), channel_id=1, source_target_pairs={{0,16},{16,0},{1,17},{17,1},{2,18},{18,2},{3,19},{19,3},{4,20},{20... | collective-permute-start | bytes 14155784 | tf_op jit(solution)/shard_map/ppermute | solution.py:202
  184.6 163.6 %collective-permute-start.53 = (bf16[16,192,768]{2,1,0:T(8,128)(2,1)}, bf16[16,192,768]{2,1,0:T(8,128)(2,1)}, u32[]{:S(2)}, u32[]{:S(2)}) collective-permute-start(bf16[16,192,768]{2,1,0:T(8,128)(2,1)} %pad_maximum_fusion.1), channel_id=1, source_target_pairs={{0,16},{16,0},{1,17},{17,1},{2,18},{18,2},{3,19},{19,3},{4,20},{20... | collective-permute-start | bytes 14155784 | tf_op jit(solution)/shard_map/ppermute | solution.py:202
  465.5 72.0 %collective-permute-start.54 = (bf16[512,768]{1,0:T(8,128)(2,1)}, bf16[512,768]{1,0:T(8,128)(2,1)}, u32[]{:S(2)}, u32[]{:S(2)}) collective-permute-start(bf16[512,768]{1,0:T(8,128)(2,1)} %get-tuple-element.108), channel_id=1, source_target_pairs={{0,16},{16,0},{1,17},{17,1},{2,18},{18,2},{3,19},{19,3},{4,20},{20... | collective-permute-start | bytes 2359304 | tf_op jit(solution)/shard_map/ppermute | solution.py:202
  500.2 40.4 %collective-permute-start.55 = (f32[512,768]{1,0:T(8,128)}, f32[512,768]{1,0:T(8,128)}, u32[]{:S(2)}, u32[]{:S(2)}) collective-permute-start(f32[512,768]{1,0:T(8,128)} %fusion.95), channel_id=1, source_target_pairs={{0,16},{16,0},{1,17},{17,1},{2,18},{18,2},{3,19},{19,3},{4,20},{20... | collective-permute-start | bytes 4718600 | tf_op jit(solution)/shard_map/ppermute | solution.py:202
  507.5 36.7 %collective-permute-start.56 = (bf16[16,112,768]{2,1,0:T(8,128)(2,1)}, bf16[16,112,768]{2,1,0:T(8,128)(2,1)}, u32[]{:S(2)}, u32[]{:S(2)}) collective-permute-start(bf16[16,112,768]{2,1,0:T(8,128)(2,1)} %get-tuple-element.224), channel_id=1, source_target_pairs={{0,16},{16,0},{1,17},{17,1},{2,18},{18,2},{3,19},{19,3},{4,20},{20... | collective-permute-start | bytes 8257544 | tf_op jit(solution)/shard_map/ppermute | solution.py:202
  508.4 35.8 %collective-permute-start.69 = (bf16[16,112,768]{2,1,0:T(8,128)(2,1)}, bf16[16,112,768]{2,1,0:T(8,128)(2,1)}, u32[]{:S(2)}, u32[]{:S(2)}) collective-permute-start(bf16[16,112,768]{2,1,0:T(8,128)(2,1)} %get-tuple-element.225), channel_id=1, source_target_pairs={{0,16},{16,0},{1,17},{17,1},{2,18},{18,2},{3,19},{19,3},{4,20},{20... | collective-permute-start | bytes 8257544 | tf_op jit(solution)/shard_map/ppermute | solution.py:202
  533.9 103.6 %collective-permute-start.96 = (bf16[16,192,768]{2,1,0:T(8,128)(2,1)}, bf16[16,192,768]{2,1,0:T(8,128)(2,1)}, u32[]{:S(2)}, u32[]{:S(2)}) collective-permute-start(bf16[16,192,768]{2,1,0:T(8,128)(2,1)} %bitcast_select_fusion), channel_id=1, source_target_pairs={{0,16},{16,0},{1,17},{17,1},{2,18},{18,2},{3,19},{19,3},{4,20},{20... | collective-permute-start | bytes 14155784 | tf_op jit(solution)/shard_map/ppermute | solution.py:202
  537.5 113.1 %collective-permute-start.83 = (bf16[16,192,768]{2,1,0:T(8,128)(2,1)}, bf16[16,192,768]{2,1,0:T(8,128)(2,1)}, u32[]{:S(2)}, u32[]{:S(2)}) collective-permute-start(bf16[16,192,768]{2,1,0:T(8,128)(2,1)} %bitcast_select_fusion.2), channel_id=1, source_target_pairs={{0,16},{16,0},{1,17},{17,1},{2,18},{18,2},{3,19},{19,3},{4,20},{20... | collective-permute-start | bytes 14155784 | tf_op jit(solution)/shard_map/ppermute | solution.py:202
  552.8 20.2 %collective-permute-start.57 = (bf16[2,2,2,1,40,768]{5,4,3,2,1,0:T(8,128)(2,1)S(1)}, bf16[2,2,2,1,40,768]{5,4,3,2,1,0:T(8,128)(2,1)S(1)}, u32[]{:S(2)}, u32[]{:S(2)}) collective-permute-start(bf16[2,2,2,1,40,768]{5,4,3,2,1,0:T(8,128)(2,1)S(1)} %constant_dynamic-slice_fusion.47), channel_id=1, source_target_pairs={{0,1},{1,0},{2,3},{3,2},{4,5},{5,4},{6,7},{7,6},{8,9},{9,8},{10,11... | collective-permute-start | bytes 1474568 | tf_op jit(solution)/shard_map/ppermute | solution.py:218
  554.2 17.3 %collective-permute-start.78 = (bf16[2,1,2,2,32,768]{5,4,3,2,1,0:T(8,128)(2,1)S(1)}, bf16[2,1,2,2,32,768]{5,4,3,2,1,0:T(8,128)(2,1)S(1)}, u32[]{:S(2)}, u32[]{:S(2)}) collective-permute-start(bf16[2,1,2,2,32,768]{5,4,3,2,1,0:T(8,128)(2,1)S(1)} %constant_dynamic-slice_fusion.27), channel_id=1, source_target_pairs={{0,4},{1,5},{2,6},{3,7},{4,0},{5,1},{6,2},{7,3},{8,12},{9,13},{10,... | collective-permute-start | bytes 1179656 | tf_op jit(solution)/shard_map/ppermute | solution.py:218
  645.1 19.9 %collective-permute-start.101 = (bf16[2,2,1,2,64,768]{5,4,3,2,1,0:T(8,128)(2,1)}, bf16[2,2,1,2,64,768]{5,4,3,2,1,0:T(8,128)(2,1)}, u32[]{:S(2)}, u32[]{:S(2)}) collective-permute-start(bf16[2,2,1,2,64,768]{5,4,3,2,1,0:T(8,128)(2,1)} %constant_dynamic-slice_fusion.7), channel_id=1, source_target_pairs={{0,2},{1,3},{2,0},{3,1},{4,6},{5,7},{6,4},{7,5},{8,10},{9,11},{10,... | collective-permute-start | bytes 2359304 | tf_op jit(solution)/shard_map/ppermute | solution.py:218
  646.6 21.4 %collective-permute-start.97 = (bf16[2,2,2,1,64,768]{5,4,3,2,1,0:T(8,128)(2,1)}, bf16[2,2,2,1,64,768]{5,4,3,2,1,0:T(8,128)(2,1)}, u32[]{:S(2)}, u32[]{:S(2)}) collective-permute-start(bf16[2,2,2,1,64,768]{5,4,3,2,1,0:T(8,128)(2,1)} %constant_dynamic-slice_fusion.11), channel_id=1, source_target_pairs={{0,1},{1,0},{2,3},{3,2},{4,5},{5,4},{6,7},{7,6},{8,9},{9,8},{10,11... | collective-permute-start | bytes 2359304 | tf_op jit(solution)/shard_map/ppermute | solution.py:218
  648.7 21.2 %collective-permute-start.105 = (bf16[2,1,2,2,64,768]{5,4,3,2,1,0:T(8,128)(2,1)}, bf16[2,1,2,2,64,768]{5,4,3,2,1,0:T(8,128)(2,1)}, u32[]{:S(2)}, u32[]{:S(2)}) collective-permute-start(bf16[2,1,2,2,64,768]{5,4,3,2,1,0:T(8,128)(2,1)} %constant_dynamic-slice_fusion.3), channel_id=1, source_target_pairs={{0,4},{1,5},{2,6},{3,7},{4,0},{5,1},{6,2},{7,3},{8,12},{9,13},{10,... | collective-permute-start | bytes 2359304 | tf_op jit(solution)/shard_map/ppermute | solution.py:218
  656.0 25.8 %collective-permute-start.88 = (bf16[2,2,1,2,64,768]{5,4,3,2,1,0:T(8,128)(2,1)S(1)}, bf16[2,2,1,2,64,768]{5,4,3,2,1,0:T(8,128)(2,1)S(1)}, u32[]{:S(2)}, u32[]{:S(2)}) collective-permute-start(bf16[2,2,1,2,64,768]{5,4,3,2,1,0:T(8,128)(2,1)S(1)} %constant_dynamic-slice_fusion.19), channel_id=1, source_target_pairs={{0,2},{1,3},{2,0},{3,1},{4,6},{5,7},{6,4},{7,5},{8,10},{9,11},{10,... | collective-permute-start | bytes 2359304 | tf_op jit(solution)/shard_map/ppermute | solution.py:218
  657.5 25.7 %collective-permute-start.84 = (bf16[2,2,2,1,64,768]{5,4,3,2,1,0:T(8,128)(2,1)S(1)}, bf16[2,2,2,1,64,768]{5,4,3,2,1,0:T(8,128)(2,1)S(1)}, u32[]{:S(2)}, u32[]{:S(2)}) collective-permute-start(bf16[2,2,2,1,64,768]{5,4,3,2,1,0:T(8,128)(2,1)S(1)} %constant_dynamic-slice_fusion.23), channel_id=1, source_target_pairs={{0,1},{1,0},{2,3},{3,2},{4,5},{5,4},{6,7},{7,6},{8,9},{9,8},{10,11... | collective-permute-start | bytes 2359304 | tf_op jit(solution)/shard_map/ppermute | solution.py:218
  665.0 20.5 %collective-permute-start.92 = (bf16[2,1,2,2,64,768]{5,4,3,2,1,0:T(8,128)(2,1)S(1)}, bf16[2,1,2,2,64,768]{5,4,3,2,1,0:T(8,128)(2,1)S(1)}, u32[]{:S(2)}, u32[]{:S(2)}) collective-permute-start(bf16[2,1,2,2,64,768]{5,4,3,2,1,0:T(8,128)(2,1)S(1)} %constant_dynamic-slice_fusion.15), channel_id=1, source_target_pairs={{0,4},{1,5},{2,6},{3,7},{4,0},{5,1},{6,2},{7,3},{8,12},{9,13},{10,... | collective-permute-start | bytes 2359304 | tf_op jit(solution)/shard_map/ppermute | solution.py:218
  668.0 25.9 %collective-permute-start.102 = (bf16[2,1,1,2,64,768]{5,4,3,2,1,0:T(8,128)(2,1)S(1)}, bf16[2,1,1,2,64,768]{5,4,3,2,1,0:T(8,128)(2,1)S(1)}, u32[]{:S(2)}, u32[]{:S(2)}) collective-permute-start(bf16[2,1,1,2,64,768]{5,4,3,2,1,0:T(8,128)(2,1)S(1)} %constant_dynamic-slice_fusion.6), channel_id=1, source_target_pairs={{0,4},{1,5},{2,6},{3,7},{4,0},{5,1},{6,2},{7,3},{8,12},{9,13},{10,... | collective-permute-start | bytes 1179656 | tf_op jit(solution)/shard_map/ppermute | solution.py:218
  669.9 25.1 %collective-permute-start.98 = (bf16[2,2,1,1,64,768]{5,4,3,2,1,0:T(8,128)(2,1)S(1)}, bf16[2,2,1,1,64,768]{5,4,3,2,1,0:T(8,128)(2,1)S(1)}, u32[]{:S(2)}, u32[]{:S(2)}) collective-permute-start(bf16[2,2,1,1,64,768]{5,4,3,2,1,0:T(8,128)(2,1)S(1)} %constant_dynamic-slice_fusion.10), channel_id=1, source_target_pairs={{0,2},{1,3},{2,0},{3,1},{4,6},{5,7},{6,4},{7,5},{8,10},{9,11},{10,... | collective-permute-start | bytes 1179656 | tf_op jit(solution)/shard_map/ppermute | solution.py:218
  683.2 19.1 %collective-permute-start.89 = (bf16[2,1,1,2,64,768]{5,4,3,2,1,0:T(8,128)(2,1)S(1)}, bf16[2,1,1,2,64,768]{5,4,3,2,1,0:T(8,128)(2,1)S(1)}, u32[]{:S(2)}, u32[]{:S(2)}) collective-permute-start(bf16[2,1,1,2,64,768]{5,4,3,2,1,0:T(8,128)(2,1)S(1)} %constant_dynamic-slice_fusion.18), channel_id=1, source_target_pairs={{0,4},{1,5},{2,6},{3,7},{4,0},{5,1},{6,2},{7,3},{8,12},{9,13},{10,... | collective-permute-start | bytes 1179656 | tf_op jit(solution)/shard_map/ppermute | solution.py:218
  685.5 18.6 %collective-permute-start.85 = (bf16[2,2,1,1,64,768]{5,4,3,2,1,0:T(8,128)(2,1)S(1)}, bf16[2,2,1,1,64,768]{5,4,3,2,1,0:T(8,128)(2,1)S(1)}, u32[]{:S(2)}, u32[]{:S(2)}) collective-permute-start(bf16[2,2,1,1,64,768]{5,4,3,2,1,0:T(8,128)(2,1)S(1)} %constant_dynamic-slice_fusion.22), channel_id=1, source_target_pairs={{0,2},{1,3},{2,0},{3,1},{4,6},{5,7},{6,4},{7,5},{8,10},{9,11},{10,... | collective-permute-start | bytes 1179656 | tf_op jit(solution)/shard_map/ppermute | solution.py:218
  711.6 17.1 %collective-permute-start.104 = (bf16[1,1,1,1,64,768]{5,4,3,2,1,0:T(8,128)(2,1)S(1)}, bf16[1,1,1,1,64,768]{5,4,3,2,1,0:T(8,128)(2,1)S(1)}, u32[]{:S(2)}, u32[]{:S(2)}) collective-permute-start(bf16[1,1,1,1,64,768]{5,4,3,2,1,0:T(8,128)(2,1)S(1)} %constant_dynamic-slice_fusion.4), channel_id=1, source_target_pairs={{0,8},{1,9},{2,10},{3,11},{4,12},{5,13},{6,14},{7,15},{8,0},{9,1},... | collective-permute-start | bytes 294920 | tf_op jit(solution)/shard_map/ppermute | solution.py:218
  713.1 17.7 %collective-permute-start.100 = (bf16[1,1,1,1,64,768]{5,4,3,2,1,0:T(8,128)(2,1)S(1)}, bf16[1,1,1,1,64,768]{5,4,3,2,1,0:T(8,128)(2,1)S(1)}, u32[]{:S(2)}, u32[]{:S(2)}) collective-permute-start(bf16[1,1,1,1,64,768]{5,4,3,2,1,0:T(8,128)(2,1)S(1)} %constant_dynamic-slice_fusion.8), channel_id=1, source_target_pairs={{0,8},{1,9},{2,10},{3,11},{4,12},{5,13},{6,14},{7,15},{8,0},{9,1},... | collective-permute-start | bytes 294920 | tf_op jit(solution)/shard_map/ppermute | solution.py:218
  714.8 20.2 %collective-permute-start.108 = (bf16[1,1,1,1,64,768]{5,4,3,2,1,0:T(8,128)(2,1)S(1)}, bf16[1,1,1,1,64,768]{5,4,3,2,1,0:T(8,128)(2,1)S(1)}, u32[]{:S(2)}, u32[]{:S(2)}) collective-permute-start(bf16[1,1,1,1,64,768]{5,4,3,2,1,0:T(8,128)(2,1)S(1)} %constant_dynamic-slice_fusion), channel_id=1, source_target_pairs={{0,8},{1,9},{2,10},{3,11},{4,12},{5,13},{6,14},{7,15},{8,0},{9,1},... | collective-permute-start | bytes 294920 | tf_op jit(solution)/shard_map/ppermute | solution.py:218
  716.3 20.8 %collective-permute-start.91 = (bf16[1,1,1,1,64,768]{5,4,3,2,1,0:T(8,128)(2,1)S(1)}, bf16[1,1,1,1,64,768]{5,4,3,2,1,0:T(8,128)(2,1)S(1)}, u32[]{:S(2)}, u32[]{:S(2)}) collective-permute-start(bf16[1,1,1,1,64,768]{5,4,3,2,1,0:T(8,128)(2,1)S(1)} %constant_dynamic-slice_fusion.16), channel_id=1, source_target_pairs={{0,8},{1,9},{2,10},{3,11},{4,12},{5,13},{6,14},{7,15},{8,0},{9,1},... | collective-permute-start | bytes 294920 | tf_op jit(solution)/shard_map/ppermute | solution.py:218
  718.0 21.2 %collective-permute-start.87 = (bf16[1,1,1,1,64,768]{5,4,3,2,1,0:T(8,128)(2,1)S(1)}, bf16[1,1,1,1,64,768]{5,4,3,2,1,0:T(8,128)(2,1)S(1)}, u32[]{:S(2)}, u32[]{:S(2)}) collective-permute-start(bf16[1,1,1,1,64,768]{5,4,3,2,1,0:T(8,128)(2,1)S(1)} %constant_dynamic-slice_fusion.20), channel_id=1, source_target_pairs={{0,8},{1,9},{2,10},{3,11},{4,12},{5,13},{6,14},{7,15},{8,0},{9,1},... | collective-permute-start | bytes 294920 | tf_op jit(solution)/shard_map/ppermute | solution.py:218
  (209 other events, 2105.0 us)

commit v3 on v2

--- a/solution.py
+++ b/solution.py
@@ -279,7 +279,9 @@
     for size in units:
         small.append(vectors[:, at : at + size * rows].reshape(size * width))
         at += size * rows
-    up = up.reshape(count, -1, rows, width).transpose(0, 2, 1, 3).reshape(width, -1)
+    up = jnp.concatenate(
+        [square(up[:, at : at + rows]) for at in range(0, up.shape[1], rows)], axis=1
+    )
     down = down.reshape(-1, width)
     return ((query, key, value), out, up, down, *small)
 
@@ -290,29 +292,33 @@
     return flat.reshape(count, VECTOR_ROWS, width)
 
 
-def reduce_pair(low, high, core):
+def pair_total(low, high, core):
     arrived = swap(jnp.where(core == 0, high, low))
     own = jnp.where(core == 0, low, high)
-    total = (own.astype(jnp.float32) + arrived.astype(jnp.float32)).astype(jnp.bfloat16)
-    return scatter_sum_dp(total, total.shape[0])
-
-
-def reduce_mlp(grads, core, count, width):
+    return (own.astype(jnp.float32) + arrived.astype(jnp.float32)).astype(jnp.bfloat16)
+
+
+def mlp_pair(grads, count, width):
     rows = width // count
-    up = grads[2].astype(jnp.bfloat16).reshape(count, rows, -1, width)
-    up = up.transpose(0, 2, 1, 3).reshape(count, -1, width)
+    up = jnp.concatenate(
+        [
+            block.reshape(count, rows, width)
+            for block in jnp.split(grads[2].astype(jnp.bfloat16), grads[2].shape[1] // width, axis=1)
+        ],
+        axis=1,
+    )
     down = grads[3].astype(jnp.bfloat16).reshape(count, -1, width)
-    return reduce_pair(up, down, core)
-
-
-def reduce_attn(grads, core, count, width):
+    return up, down
+
+
+def attn_pair(grads, count, width):
     rows = width // count
     query, key, value = (part.astype(jnp.bfloat16).reshape(count, rows, width) for part in grads[0])
     out = grads[1].astype(jnp.bfloat16).reshape(count, rows, width)
     small = pack_vectors([vector.astype(jnp.bfloat16) for vector in grads[4:]], count, width)
     low = jnp.concatenate([query, key, small], axis=1)
     high = jnp.concatenate([value, out, jnp.zeros_like(small)], axis=1)
-    return reduce_pair(low, high, core)
+    return low, high
 
 
 def on_device(
@@ -390,9 +396,17 @@
     for layer in (1, 0):
         d_entry, grads = layer_backward(upstream, entries[layer], keeps[layer], parameters[layer])
         backs[layer] = d_entry
-        mlps[layer] = reduce_mlp(grads, core, count, width)
-        attns[layer] = reduce_attn(grads, core, count, width)
-        upstream = d_entry.astype(jnp.bfloat16).astype(jnp.float32)
+        upstream = d_entry.astype(jnp.bfloat16)
+        if layer:
+            upstream, totals = lax.optimization_barrier(
+                (upstream, (pair_total(*mlp_pair(grads, count, width), core),
+                            pair_total(*attn_pair(grads, count, width), core)))
+            )
+        else:
+            totals = (pair_total(*mlp_pair(grads, count, width), core),
+                      pair_total(*attn_pair(grads, count, width), core))
+        mlps[layer], attns[layer] = (scatter_sum_dp(total, count) for total in totals)
+        upstream = upstream.astype(jnp.float32)
     input_grads = by_layer(*backs)
     mlp_low, mlp_high = by_layer(*mlps).astype(jnp.float32)
     attn_low, attn_high = by_layer(*attns).astype(jnp.float32)

time: 755 us -> 745 us (0.987)
  local copies, waits for them, and re-layouts: 107 us -> 85.8 us
    reshape x5 -> x0, local copies, waits for them, and re-layouts: 27.9 us -> none  [the longest x3 23.1 us: reduce_mlp(): up = grads[2].astype(jnp.bfloat16).reshape(count, rows, -1, width)]
    dot_general x2, matrix products: 7.99 us -> 17.9 us  [layer_forward(): jnp.einsum('hts,shd->thd', weights, values, preferred_element_type=jnp.fl...]
    unnamed x300 -> x410, local copies, waits for them, and re-layouts: 12.7 us -> 18 us
    convert_element_type x3 -> x5, other arithmetic: 15.6 us -> 17.8 us  [the longest x4 15.7 us: pair_total(): (own.astype(jnp.float32) + arrived.astype(jnp.float32)).astype(jnp.bfloat16)]
  transfers between devices with their start and end apart: 110 -> 110, of which waited for: 49 -> 58; matrix products, arithmetic and copies ran while one was open for 38% -> 32% of each run, Pallas kernels for 0% -> 0%
where the time goes in v3:
time: 745 us; the launch traced here: 739 us
  matrix products  203 us (27%)
  waiting for transfers between devices  200 us (27%)
  starting transfers between devices  132 us (18%)
  other arithmetic  113 us (15%)
  local copies, waits for them, and re-layouts  85.8 us (12%)
    ppermute x96, waiting for transfers between devices, exchange(): lax.ppermute(value, 'dp', [(source, source ^ 1 << bit) for source in rang...  199 us
    ppermute x96, starting transfers between devices, exchange(): lax.ppermute(value, 'dp', [(source, source ^ 1 << bit) for source in rang...  130 us
    dot_general x2, matrix products, layer_forward(): jnp.dot(normed_m, up_w, preferred_element_type=jnp.float32)  40.6 us
    dot_general x2, matrix products, layer_backward(): jnp.einsum('td,fd->tf', up_low, down_w, preferred_element_type=jnp.float32)  18.8 us
    dot_general x6, matrix products, layer_forward(): jnp.dot(normed_a, part, preferred_element_type=jnp.float32)  18.3 us
    unnamed x410, local copies, waits for them, and re-layouts  18 us
    dot_general x2, matrix products, layer_forward(): jnp.einsum('hts,shd->thd', weights, values, preferred_element_type=jnp.fl...  17.9 us
    dot_general x2, matrix products, layer_backward(): jnp.einsum('thd,shd->hts', d_attended, values, preferred_element_type=jnp...  16.7 us
  transfers between devices with their start and end apart: 110, of which 58 were waited for; matrix products, arithmetic and copies ran while one was open for 32% of the time, Pallas kernels for 0%

profile of v3, /device:TPU:0, one launch (start us, length us, event | category | flops | bytes accessed | tf_op | source)
XLA Modules:
  0.0 738.6 jit_solution(13189978144106325932)
XLA Ops:
  12.0 4.0 collective-permute-start.9
  21.9 5.5 collective-permute-done.36
  32.5 4.1 collective-permute-start.2
  47.4 9.7 %collective-permute-done.19 = bf16[1,1,1,1,64,768]{5,4,3,2,1,0:T(8,128)(2,1)S(1)} collective-permute-done((bf16[1,1,1,1,64,768]{5,4,3,2,1,0:T(8,128)(2,1)S(1)}, bf16[1,1,1,1,64,768]{5,4,3,2,1,0:T(8,128)(2,1)S(1)}, u32[]{:S(2)}, u32[]{:S(2)}) %collective-permute-start.19) | collective-permute-done | bytes 98336 | tf_op jit(solution)/shard_map/ppermute | solution.py:218
  57.1 5.2 collective-permute-done.49
  82.6 5.2 collective-permute-start.46
  88.3 3.5 collective-permute-done.46
  110.9 3.8 collective-permute-start.4
  114.8 3.6 collective-permute-done.21
  134.7 7.8 %collective-permute-done.35 = bf16[2,2,1,2,40,768]{5,4,3,2,1,0:T(8,128)(2,1)S(1)} collective-permute-done((bf16[2,2,1,2,40,768]{5,4,3,2,1,0:T(8,128)(2,1)S(1)}, bf16[2,2,1,2,40,768]{5,4,3,2,1,0:T(8,128)(2,1)S(1)}, u32[]{:S(2)}, u32[]{:S(2)}) %collective-permute-start.35) | collective-permute-done | bytes 491552 | tf_op jit(solution)/shard_map/ppermute | solution.py:218
  145.1 7.3 collective-permute-done.26
  152.6 6.1 collective-permute-done.22
  167.9 10.0 %collective-permute-done.48 = bf16[2,2,1,2,64,768]{5,4,3,2,1,0:T(8,128)(2,1)S(1)} collective-permute-done((bf16[2,2,1,2,64,768]{5,4,3,2,1,0:T(8,128)(2,1)S(1)}, bf16[2,2,1,2,64,768]{5,4,3,2,1,0:T(8,128)(2,1)S(1)}, u32[]{:S(2)}, u32[]{:S(2)}) %collective-permute-start.48) | collective-permute-done | bytes 786464 | tf_op jit(solution)/shard_map/ppermute | solution.py:218
  205.2 3.6 convolution_add_fusion.2
  214.0 3.6 convolution_add_fusion.3
  245.8 13.5 %fusion.78 = bf16[12,64,512]{2,1,0:T(8,128)(2,1)S(1)} fusion(bf16[512,12,64]{0,2,1:T(8,128)(2,1)} %bitcast.614, f32[12,512]{1,0:T(8,128)S(1)} %fusion, f32[12,512]{1,0:T(8,128)S(1)} %get-tuple-element.243, f32[12,512,512]{1,2,0:T(8,128)S(1)} %get-tuple-element.244, pred[512,512]{0,1:T(8,128)(4,1)S(1)} %compare_and_fusion), kind=kOutput, calls=%fused_computation.190 | convolution fusion | flops 418775040 | bytes 14467072 | tf_op jit(solution)/shard_map/hts,shd->thd/dot_general | solution.py:84
  261.0 4.1 broadcast_select_fusion.4
  267.8 20.3 %multiply_convert_fusion.3 = (bf16[512,3072]{1,0:T(8,128)(2,1)S(1)}, f32[512,3072]{1,0:T(8,128)}, f32[512,3072]{1,0:T(8,128)}) fusion(f32[3072]{0:T(1024)S(1)} %copy-done.159, bf16[768,768]{1,0:T(8,128)(2,1)S(1)} %bitcast.638, bf16[768,768]{1,0:T(8,128)(2,1)S(1)} %bitcast.640, bf16[768,768]{1,0:T(8,128)(2,1)S(1)} %bitcast.642, ...), kind=kOutput, calls=%fused_computation.41 | convolution fusion | flops 2540961792 | bytes 21258244 | tf_op jit(solution)/shard_map/dot_general | solution.py:86
  295.4 4.0 convolution_add_fusion.1
  314.0 7.2 multiply_reduce_fusion.1
  321.2 7.0 multiply_convert_fusion.1
  334.3 4.6 bitcast_reduce_fusion.1
  339.0 4.4 fusion.77
  343.4 4.2 broadcast_select_fusion.2
  348.4 20.3 %multiply_convert_fusion.2 = (bf16[512,3072]{1,0:T(8,128)(2,1)S(1)}, f32[512,3072]{1,0:T(8,128)}, f32[512,3072]{1,0:T(8,128)}) fusion(f32[3072]{0:T(1024)S(1)} %copy-done.161, bf16[768,768]{1,0:T(8,128)(2,1)S(1)} %bitcast.646, bf16[768,768]{1,0:T(8,128)(2,1)S(1)} %bitcast.648, bf16[768,768]{1,0:T(8,128)(2,1)S(1)} %bitcast.650, ...), kind=kOutput, calls=%fused_computation.28 | convolution fusion | flops 2540961792 | bytes 21256192 | tf_op jit(solution)/shard_map/dot_general | solution.py:86
  368.7 10.2 %fusion.218 = (bf16[3072]{0:T(1024)(128)(2,1)S(1)}, bf16[512,3072]{1,0:T(8,128)(2,1)}) fusion(f32[512,3072]{1,0:T(8,128)} %get-tuple-element.59, bf16[3072,768]{1,0:T(8,128)(2,1)S(1)} %bitcast.576, bf16[2,512,768]{2,1,0:T(8,128)(2,1)S(1)} %copy-done.70, s32[]{:T(128)S(6)} %select_n.1520, f32[512,3072]{1,0:T(8,128)} %get-tuple-element.250, ...), kind=kOutput, calls=%fused_computation.637 | convolution fusion | flops 2441081856 | bytes 21252100 | tf_op jit(solution)/shard_map/td,fd->tf/dot_general | solution.py:136
  378.9 4.7 fusion.79
  405.8 3.6 fusion.194
  422.3 5.2 broadcast_select_fusion.14
  433.3 3.7 add_convert_fusion.5
  437.1 6.8 add_convert_fusion.1
  447.9 9.6 %bitcast_reduce_fusion = (bf16[12,64]{1,0:T(8,128)(2,1)}, bf16[12,64,512]{2,1,0:T(8,128)(2,1)}) fusion(bf16[512,12,64]{0,2,1:T(8,128)(2,1)} %bitcast.620, f32[12,512]{1,0:T(8,128)S(1)} %log_add_fusion, f32[12,512,512]{1,2,0:T(8,128)} %copy-done, pred[512,512]{0,1:T(8,128)(4,1)S(1)} %compare_and_fusion), kind=kOutput, calls=%fused_computation.228 | convolution fusion | flops 416021760 | bytes 14444032 | tf_op jit(solution)/shard_map/hts,thd->shd/dot_general | solution.py:148
  457.5 9.5 %multiply_reduce_fusion = (f32[12,512]{1,0:T(8,128)S(1)}, f32[12,512,512]{1,2,0:T(8,128)}) fusion(f32[12,512]{1,0:T(8,128)S(1)} %log_add_fusion, f32[12,512,512]{1,2,0:T(8,128)} %copy-done, pred[512,512]{0,1:T(8,128)(4,1)S(1)} %compare_and_fusion, bf16[512,12,64]{0,2,1:T(8,128)(2,1)S(1)} %bitcast.621, bf16[512,12,64]{0,2,1:T(8,128)(2,1)S(1)} %bitcast.615), kind=kOutput, calls=%fused_computation.1 | convolution fusion | flops 418375680 | bytes 27049984 | tf_op jit(solution)/shard_map/thd,shd->hts/dot_general | solution.py:147
  467.1 7.3 multiply_convert_fusion
  498.0 4.4 convolution_convert_fusion
  502.4 8.6 %fusion.195 = (bf16[3072]{0:T(1024)(128)(2,1)}, bf16[512,3072]{1,0:T(8,128)(2,1)S(1)}) fusion(f32[512,3072]{1,0:T(8,128)} %get-tuple-element.61, f32[512,3072]{1,0:T(8,128)} %get-tuple-element.245, f32[3072]{0:T(1024)S(1)} %copy-done.160, bf16[512,768]{1,0:T(8,128)(2,1)S(1)} %copy-done.22, bf16[3072,768]{1,0:T(8,128)(2,1)S(1)} %bitcast.575), kind=kOutput, calls=%fused_computation.616 | convolution fusion | flops 2441081856 | bytes 21252096 | tf_op jit(solution)/shard_map/td,fd->tf/dot_general | solution.py:136
  511.0 4.8 convolution_convert_fusion.1
  515.9 3.6 fusion.52
  550.8 3.6 collective-permute-done.81
  555.4 9.8 %collective-permute-done.76 = bf16[2,1,1,2,40,768]{5,4,3,2,1,0:T(8,128)(2,1)S(1)} collective-permute-done((bf16[2,1,1,2,40,768]{5,4,3,2,1,0:T(8,128)(2,1)S(1)}, bf16[2,1,1,2,40,768]{5,4,3,2,1,0:T(8,128)(2,1)S(1)}, u32[]{:S(2)}, u32[]{:S(2)}) %collective-permute-start.76) | collective-permute-done | bytes 245792 | tf_op jit(solution)/shard_map/ppermute | solution.py:218
  572.1 11.3 %collective-permute-done.101 = bf16[2,2,1,2,64,768]{5,4,3,2,1,0:T(8,128)(2,1)S(1)} collective-permute-done((bf16[2,2,1,2,64,768]{5,4,3,2,1,0:T(8,128)(2,1)S(1)}, bf16[2,2,1,2,64,768]{5,4,3,2,1,0:T(8,128)(2,1)S(1)}, u32[]{:S(2)}, u32[]{:S(2)}) %collective-permute-start.101) | collective-permute-done | bytes 786464 | tf_op jit(solution)/shard_map/ppermute | solution.py:218
  584.0 5.5 collective-permute-done.97
  607.3 7.6 %collective-permute-done.102 = bf16[2,1,1,2,64,768]{5,4,3,2,1,0:T(8,128)(2,1)S(1)} collective-permute-done((bf16[2,1,1,2,64,768]{5,4,3,2,1,0:T(8,128)(2,1)S(1)}, bf16[2,1,1,2,64,768]{5,4,3,2,1,0:T(8,128)(2,1)S(1)}, u32[]{:S(2)}, u32[]{:S(2)}) %collective-permute-start.102) | collective-permute-done | bytes 393248 | tf_op jit(solution)/shard_map/ppermute | solution.py:218
  616.6 4.0 collective-permute-done.107
  647.2 4.5 collective-permute-done.63
  685.9 14.4 %collective-permute-done.93 = bf16[2,1,2,2,64,768]{5,4,3,2,1,0:T(8,128)(2,1)} collective-permute-done((bf16[2,1,2,2,64,768]{5,4,3,2,1,0:T(8,128)(2,1)}, bf16[2,1,2,2,64,768]{5,4,3,2,1,0:T(8,128)(2,1)}, u32[]{:S(2)}, u32[]{:S(2)}) %collective-permute-start.93) | collective-permute-done | bytes 786464 | tf_op jit(solution)/shard_map/ppermute | solution.py:218
  706.5 5.9 collective-permute-done.94
  725.2 6.6 collective-permute-done.96
  (978 shorter events, 406.4 us)
Async XLA Ops:
  7.0 29.8 %collective-permute-start.14 = (bf16[192,768]{1,0:T(8,128)(2,1)}, bf16[192,768]{1,0:T(8,128)(2,1)}, u32[]{:S(2)}, u32[]{:S(2)}) collective-permute-start(bf16[192,768]{1,0:T(8,128)(2,1)} %bitcast_select_fusion), channel_id=1, source_target_pairs={{0,16},{16,0},{1,17},{17,1},{2,18},{18,2},{3,19},{19,3},{4,20},{20... | collective-permute-start | bytes 884744 | tf_op jit(solution)/shard_map/ppermute | solution.py:202
  16.0 13.2 %collective-permute-start.5 = (bf16[1,1,1,1,40,768]{5,4,3,2,1,0:T(8,128)(2,1)S(1)}, bf16[1,1,1,1,40,768]{5,4,3,2,1,0:T(8,128)(2,1)S(1)}, u32[]{:S(2)}, u32[]{:S(2)}) collective-permute-start(bf16[1,1,1,1,40,768]{5,4,3,2,1,0:T(8,128)(2,1)S(1)} %get-tuple-element.196), channel_id=1, source_target_pairs={{0,8},{1,9},{2,10},{3,11},{4,12},{5,13},{6,14},{7,15},{8,0},{9,1},... | collective-permute-start | bytes 184328 | tf_op jit(solution)/shard_map/ppermute | solution.py:218
  38.7 26.0 %collective-permute-start.23 = (bf16[1,1,1,1,64,768]{5,4,3,2,1,0:T(8,128)(2,1)S(1)}, bf16[1,1,1,1,64,768]{5,4,3,2,1,0:T(8,128)(2,1)S(1)}, u32[]{:S(2)}, u32[]{:S(2)}) collective-permute-start(bf16[1,1,1,1,64,768]{5,4,3,2,1,0:T(8,128)(2,1)S(1)} %get-tuple-element.163), channel_id=1, source_target_pairs={{0,8},{1,9},{2,10},{3,11},{4,12},{5,13},{6,14},{7,15},{8,0},{9,1},... | collective-permute-start | bytes 294920 | tf_op jit(solution)/shard_map/ppermute | solution.py:218
  40.9 16.2 %collective-permute-start.19 = (bf16[1,1,1,1,64,768]{5,4,3,2,1,0:T(8,128)(2,1)S(1)}, bf16[1,1,1,1,64,768]{5,4,3,2,1,0:T(8,128)(2,1)S(1)}, u32[]{:S(2)}, u32[]{:S(2)}) collective-permute-start(bf16[1,1,1,1,64,768]{5,4,3,2,1,0:T(8,128)(2,1)S(1)} %get-tuple-element.162), channel_id=1, source_target_pairs={{0,8},{1,9},{2,10},{3,11},{4,12},{5,13},{6,14},{7,15},{8,0},{9,1},... | collective-permute-start | bytes 294920 | tf_op jit(solution)/shard_map/ppermute | solution.py:218
  41.9 22.9 %collective-permute-start.15 = (bf16[1,1,1,1,64,768]{5,4,3,2,1,0:T(8,128)(2,1)S(1)}, bf16[1,1,1,1,64,768]{5,4,3,2,1,0:T(8,128)(2,1)S(1)}, u32[]{:S(2)}, u32[]{:S(2)}) collective-permute-start(bf16[1,1,1,1,64,768]{5,4,3,2,1,0:T(8,128)(2,1)S(1)} %get-tuple-element.161), channel_id=1, source_target_pairs={{0,8},{1,9},{2,10},{3,11},{4,12},{5,13},{6,14},{7,15},{8,0},{9,1},... | collective-permute-start | bytes 294920 | tf_op jit(solution)/shard_map/ppermute | solution.py:218
  44.1 18.3 %collective-permute-start.49 = (bf16[1,1,1,1,64,768]{5,4,3,2,1,0:T(8,128)(2,1)S(1)}, bf16[1,1,1,1,64,768]{5,4,3,2,1,0:T(8,128)(2,1)S(1)}, u32[]{:S(2)}, u32[]{:S(2)}) collective-permute-start(bf16[1,1,1,1,64,768]{5,4,3,2,1,0:T(8,128)(2,1)S(1)} %get-tuple-element.157), channel_id=1, source_target_pairs={{0,8},{1,9},{2,10},{3,11},{4,12},{5,13},{6,14},{7,15},{8,0},{9,1},... | collective-permute-start | bytes 294920 | tf_op jit(solution)/shard_map/ppermute | solution.py:218
  45.1 20.8 %collective-permute-start.45 = (bf16[1,1,1,1,64,768]{5,4,3,2,1,0:T(8,128)(2,1)S(1)}, bf16[1,1,1,1,64,768]{5,4,3,2,1,0:T(8,128)(2,1)S(1)}, u32[]{:S(2)}, u32[]{:S(2)}) collective-permute-start(bf16[1,1,1,1,64,768]{5,4,3,2,1,0:T(8,128)(2,1)S(1)} %get-tuple-element.156), channel_id=1, source_target_pairs={{0,8},{1,9},{2,10},{3,11},{4,12},{5,13},{6,14},{7,15},{8,0},{9,1},... | collective-permute-start | bytes 294920 | tf_op jit(solution)/shard_map/ppermute | solution.py:218
  64.8 31.8 %collective-permute-start.7 = (bf16[2,1,1,2,40,768]{5,4,3,2,1,0:T(8,128)(2,1)S(1)}, bf16[2,1,1,2,40,768]{5,4,3,2,1,0:T(8,128)(2,1)S(1)}, u32[]{:S(2)}, u32[]{:S(2)}) collective-permute-start(bf16[2,1,1,2,40,768]{5,4,3,2,1,0:T(8,128)(2,1)S(1)} %maximum_select_fusion.39), channel_id=1, source_target_pairs={{0,4},{1,5},{2,6},{3,7},{4,0},{5,1},{6,2},{7,3},{8,12},{9,13},{10,... | collective-permute-start | bytes 737288 | tf_op jit(solution)/shard_map/ppermute | solution.py:218
  65.9 37.8 %collective-permute-start.3 = (bf16[2,2,1,1,40,768]{5,4,3,2,1,0:T(8,128)(2,1)S(1)}, bf16[2,2,1,1,40,768]{5,4,3,2,1,0:T(8,128)(2,1)S(1)}, u32[]{:S(2)}, u32[]{:S(2)}) collective-permute-start(bf16[2,2,1,1,40,768]{5,4,3,2,1,0:T(8,128)(2,1)S(1)} %maximum_select_fusion.37), channel_id=1, source_target_pairs={{0,2},{1,3},{2,0},{3,1},{4,6},{5,7},{6,4},{7,5},{8,10},{9,11},{10,... | collective-permute-start | bytes 737288 | tf_op jit(solution)/shard_map/ppermute | solution.py:218
  67.7 36.2 %collective-permute-start.34 = (bf16[2,1,1,2,40,768]{5,4,3,2,1,0:T(8,128)(2,1)S(1)}, bf16[2,1,1,2,40,768]{5,4,3,2,1,0:T(8,128)(2,1)S(1)}, u32[]{:S(2)}, u32[]{:S(2)}) collective-permute-start(bf16[2,1,1,2,40,768]{5,4,3,2,1,0:T(8,128)(2,1)S(1)} %maximum_select_fusion.43), channel_id=1, source_target_pairs={{0,4},{1,5},{2,6},{3,7},{4,0},{5,1},{6,2},{7,3},{8,12},{9,13},{10,... | collective-permute-start | bytes 737288 | tf_op jit(solution)/shard_map/ppermute | solution.py:218
  96.6 14.3 %collective-permute-start.39 = (bf16[2,1,2,2,32,768]{5,4,3,2,1,0:T(8,128)(2,1)S(1)}, bf16[2,1,2,2,32,768]{5,4,3,2,1,0:T(8,128)(2,1)S(1)}, u32[]{:S(2)}, u32[]{:S(2)}) collective-permute-start(bf16[2,1,2,2,32,768]{5,4,3,2,1,0:T(8,128)(2,1)S(1)} %maximum_select_fusion.29), channel_id=1, source_target_pairs={{0,4},{1,5},{2,6},{3,7},{4,0},{5,1},{6,2},{7,3},{8,12},{9,13},{10,... | collective-permute-start | bytes 1179656 | tf_op jit(solution)/shard_map/ppermute | solution.py:218
  101.5 26.3 %collective-permute-start.25 = (bf16[2,1,2,1,64,768]{5,4,3,2,1,0:T(8,128)(2,1)S(1)}, bf16[2,1,2,1,64,768]{5,4,3,2,1,0:T(8,128)(2,1)S(1)}, u32[]{:S(2)}, u32[]{:S(2)}) collective-permute-start(bf16[2,1,2,1,64,768]{5,4,3,2,1,0:T(8,128)(2,1)S(1)} %maximum_select_fusion.28), channel_id=1, source_target_pairs={{0,1},{1,0},{2,3},{3,2},{4,5},{5,4},{6,7},{7,6},{8,9},{9,8},{10,11... | collective-permute-start | bytes 1179656 | tf_op jit(solution)/shard_map/ppermute | solution.py:218
  103.7 14.7 %collective-permute-start.21 = (bf16[2,1,1,2,64,768]{5,4,3,2,1,0:T(8,128)(2,1)S(1)}, bf16[2,1,1,2,64,768]{5,4,3,2,1,0:T(8,128)(2,1)S(1)}, u32[]{:S(2)}, u32[]{:S(2)}) collective-permute-start(bf16[2,1,1,2,64,768]{5,4,3,2,1,0:T(8,128)(2,1)S(1)} %maximum_select_fusion.26), channel_id=1, source_target_pairs={{0,4},{1,5},{2,6},{3,7},{4,0},{5,1},{6,2},{7,3},{8,12},{9,13},{10,... | collective-permute-start | bytes 1179656 | tf_op jit(solution)/shard_map/ppermute | solution.py:218
  103.9 25.4 %collective-permute-start.17 = (bf16[2,2,1,1,64,768]{5,4,3,2,1,0:T(8,128)(2,1)S(1)}, bf16[2,2,1,1,64,768]{5,4,3,2,1,0:T(8,128)(2,1)S(1)}, u32[]{:S(2)}, u32[]{:S(2)}) collective-permute-start(bf16[2,2,1,1,64,768]{5,4,3,2,1,0:T(8,128)(2,1)S(1)} %maximum_select_fusion.24), channel_id=1, source_target_pairs={{0,2},{1,3},{2,0},{3,1},{4,6},{5,7},{6,4},{7,5},{8,10},{9,11},{10,... | collective-permute-start | bytes 1179656 | tf_op jit(solution)/shard_map/ppermute | solution.py:218
  106.7 15.3 %collective-permute-start.8 = (bf16[2,2,1,2,40,768]{5,4,3,2,1,0:T(8,128)(2,1)S(1)}, bf16[2,2,1,2,40,768]{5,4,3,2,1,0:T(8,128)(2,1)S(1)}, u32[]{:S(2)}, u32[]{:S(2)}) collective-permute-start(bf16[2,2,1,2,40,768]{5,4,3,2,1,0:T(8,128)(2,1)S(1)} %maximum_select_fusion.19), channel_id=1, source_target_pairs={{0,2},{1,3},{2,0},{3,1},{4,6},{5,7},{6,4},{7,5},{8,10},{9,11},{10,... | collective-permute-start | bytes 1474568 | tf_op jit(solution)/shard_map/ppermute | solution.py:218
  110.9 12.6 %collective-permute-start.4 = (bf16[2,2,2,1,40,768]{5,4,3,2,1,0:T(8,128)(2,1)S(1)}, bf16[2,2,2,1,40,768]{5,4,3,2,1,0:T(8,128)(2,1)S(1)}, u32[]{:S(2)}, u32[]{:S(2)}) collective-permute-start(bf16[2,2,2,1,40,768]{5,4,3,2,1,0:T(8,128)(2,1)S(1)} %maximum_select_fusion.18), channel_id=1, source_target_pairs={{0,1},{1,0},{2,3},{3,2},{4,5},{5,4},{6,7},{7,6},{8,9},{9,8},{10,11... | collective-permute-start | bytes 1474568 | tf_op jit(solution)/shard_map/ppermute | solution.py:218
  127.6 54.5 %collective-permute-start.13 = (bf16[16,112,768]{2,1,0:T(8,128)(2,1)S(1)}, bf16[16,112,768]{2,1,0:T(8,128)(2,1)S(1)}, u32[]{:S(2)}, u32[]{:S(2)}) collective-permute-start(bf16[16,112,768]{2,1,0:T(8,128)(2,1)S(1)} %pad_maximum_fusion.6), channel_id=1, source_target_pairs={{0,16},{16,0},{1,17},{17,1},{2,18},{18,2},{3,19},{19,3},{4,20},{20... | collective-permute-start | bytes 8257544 | tf_op jit(solution)/shard_map/ppermute | solution.py:202
  127.7 14.7 %collective-permute-start.35 = (bf16[2,2,1,2,40,768]{5,4,3,2,1,0:T(8,128)(2,1)S(1)}, bf16[2,2,1,2,40,768]{5,4,3,2,1,0:T(8,128)(2,1)S(1)}, u32[]{:S(2)}, u32[]{:S(2)}) collective-permute-start(bf16[2,2,1,2,40,768]{5,4,3,2,1,0:T(8,128)(2,1)S(1)} %maximum_select_fusion.21), channel_id=1, source_target_pairs={{0,2},{1,3},{2,0},{3,1},{4,6},{5,7},{6,4},{7,5},{8,10},{9,11},{10,... | collective-permute-start | bytes 1474568 | tf_op jit(solution)/shard_map/ppermute | solution.py:218
  129.3 14.7 %collective-permute-start.31 = (bf16[2,2,2,1,40,768]{5,4,3,2,1,0:T(8,128)(2,1)S(1)}, bf16[2,2,2,1,40,768]{5,4,3,2,1,0:T(8,128)(2,1)S(1)}, u32[]{:S(2)}, u32[]{:S(2)}) collective-permute-start(bf16[2,2,2,1,40,768]{5,4,3,2,1,0:T(8,128)(2,1)S(1)} %maximum_select_fusion.20), channel_id=1, source_target_pairs={{0,1},{1,0},{2,3},{3,2},{4,5},{5,4},{6,7},{7,6},{8,9},{9,8},{10,11... | collective-permute-start | bytes 1474568 | tf_op jit(solution)/shard_map/ppermute | solution.py:218
  131.9 20.5 %collective-permute-start.26 = (bf16[2,1,2,2,64,768]{5,4,3,2,1,0:T(8,128)(2,1)S(1)}, bf16[2,1,2,2,64,768]{5,4,3,2,1,0:T(8,128)(2,1)S(1)}, u32[]{:S(2)}, u32[]{:S(2)}) collective-permute-start(bf16[2,1,2,2,64,768]{5,4,3,2,1,0:T(8,128)(2,1)S(1)} %maximum_select_fusion.13), channel_id=1, source_target_pairs={{0,4},{1,5},{2,6},{3,7},{4,0},{5,1},{6,2},{7,3},{8,12},{9,13},{10,... | collective-permute-start | bytes 2359304 | tf_op jit(solution)/shard_map/ppermute | solution.py:218
  132.6 26.2 %collective-permute-start.22 = (bf16[2,2,1,2,64,768]{5,4,3,2,1,0:T(8,128)(2,1)S(1)}, bf16[2,2,1,2,64,768]{5,4,3,2,1,0:T(8,128)(2,1)S(1)}, u32[]{:S(2)}, u32[]{:S(2)}) collective-permute-start(bf16[2,2,1,2,64,768]{5,4,3,2,1,0:T(8,128)(2,1)S(1)} %maximum_select_fusion.12), channel_id=1, source_target_pairs={{0,2},{1,3},{2,0},{3,1},{4,6},{5,7},{6,4},{7,5},{8,10},{9,11},{10,... | collective-permute-start | bytes 2359304 | tf_op jit(solution)/shard_map/ppermute | solution.py:218
  142.4 18.7 %collective-permute-start.18 = (bf16[2,2,2,1,64,768]{5,4,3,2,1,0:T(8,128)(2,1)S(1)}, bf16[2,2,2,1,64,768]{5,4,3,2,1,0:T(8,128)(2,1)S(1)}, u32[]{:S(2)}, u32[]{:S(2)}) collective-permute-start(bf16[2,2,2,1,64,768]{5,4,3,2,1,0:T(8,128)(2,1)S(1)} %maximum_select_fusion.11), channel_id=1, source_target_pairs={{0,1},{1,0},{2,3},{3,2},{4,5},{5,4},{6,7},{7,6},{8,9},{9,8},{10,11... | collective-permute-start | bytes 2359304 | tf_op jit(solution)/shard_map/ppermute | solution.py:218
  144.1 23.6 %collective-permute-start.52 = (bf16[2,1,2,2,64,768]{5,4,3,2,1,0:T(8,128)(2,1)S(1)}, bf16[2,1,2,2,64,768]{5,4,3,2,1,0:T(8,128)(2,1)S(1)}, u32[]{:S(2)}, u32[]{:S(2)}) collective-permute-start(bf16[2,1,2,2,64,768]{5,4,3,2,1,0:T(8,128)(2,1)S(1)} %maximum_select_fusion.17), channel_id=1, source_target_pairs={{0,4},{1,5},{2,6},{3,7},{4,0},{5,1},{6,2},{7,3},{8,12},{9,13},{10,... | collective-permute-start | bytes 2359304 | tf_op jit(solution)/shard_map/ppermute | solution.py:218
  152.4 34.9 %collective-permute-start.40 = (bf16[16,112,768]{2,1,0:T(8,128)(2,1)S(1)}, bf16[16,112,768]{2,1,0:T(8,128)(2,1)S(1)}, u32[]{:S(2)}, u32[]{:S(2)}) collective-permute-start(bf16[16,112,768]{2,1,0:T(8,128)(2,1)S(1)} %pad_maximum_fusion.7), channel_id=1, source_target_pairs={{0,16},{16,0},{1,17},{17,1},{2,18},{18,2},{3,19},{19,3},{4,20},{20... | collective-permute-start | bytes 8257544 | tf_op jit(solution)/shard_map/ppermute | solution.py:202
  158.7 19.2 %collective-permute-start.48 = (bf16[2,2,1,2,64,768]{5,4,3,2,1,0:T(8,128)(2,1)S(1)}, bf16[2,2,1,2,64,768]{5,4,3,2,1,0:T(8,128)(2,1)S(1)}, u32[]{:S(2)}, u32[]{:S(2)}) collective-permute-start(bf16[2,2,1,2,64,768]{5,4,3,2,1,0:T(8,128)(2,1)S(1)} %maximum_select_fusion.16), channel_id=1, source_target_pairs={{0,2},{1,3},{2,0},{3,1},{4,6},{5,7},{6,4},{7,5},{8,10},{9,11},{10,... | collective-permute-start | bytes 2359304 | tf_op jit(solution)/shard_map/ppermute | solution.py:218
  161.1 18.2 %collective-permute-start.44 = (bf16[2,2,2,1,64,768]{5,4,3,2,1,0:T(8,128)(2,1)S(1)}, bf16[2,2,2,1,64,768]{5,4,3,2,1,0:T(8,128)(2,1)S(1)}, u32[]{:S(2)}, u32[]{:S(2)}) collective-permute-start(bf16[2,2,2,1,64,768]{5,4,3,2,1,0:T(8,128)(2,1)S(1)} %maximum_select_fusion.15), channel_id=1, source_target_pairs={{0,1},{1,0},{2,3},{3,2},{4,5},{5,4},{6,7},{7,6},{8,9},{9,8},{10,11... | collective-permute-start | bytes 2359304 | tf_op jit(solution)/shard_map/ppermute | solution.py:218
  167.6 92.6 %collective-permute-start.27 = (bf16[16,192,768]{2,1,0:T(8,128)(2,1)}, bf16[16,192,768]{2,1,0:T(8,128)(2,1)}, u32[]{:S(2)}, u32[]{:S(2)}) collective-permute-start(bf16[16,192,768]{2,1,0:T(8,128)(2,1)} %pad_maximum_fusion), channel_id=1, source_target_pairs={{0,16},{16,0},{1,17},{17,1},{2,18},{18,2},{3,19},{19,3},{4,20},{20... | collective-permute-start | bytes 14155784 | tf_op jit(solution)/shard_map/ppermute | solution.py:202
  182.1 161.3 %collective-permute-start.53 = (bf16[16,192,768]{2,1,0:T(8,128)(2,1)}, bf16[16,192,768]{2,1,0:T(8,128)(2,1)}, u32[]{:S(2)}, u32[]{:S(2)}) collective-permute-start(bf16[16,192,768]{2,1,0:T(8,128)(2,1)} %pad_maximum_fusion.2), channel_id=1, source_target_pairs={{0,16},{16,0},{1,17},{17,1},{2,18},{18,2},{3,19},{19,3},{4,20},{20... | collective-permute-start | bytes 14155784 | tf_op jit(solution)/shard_map/ppermute | solution.py:202
  402.6 34.4 %collective-permute-start.55 = (bf16[16,192,768]{2,1,0:T(8,128)(2,1)}, bf16[16,192,768]{2,1,0:T(8,128)(2,1)}, u32[]{:S(2)}, u32[]{:S(2)}) collective-permute-start(bf16[16,192,768]{2,1,0:T(8,128)(2,1)} %broadcast_select_fusion.1), channel_id=1, source_target_pairs={{0,16},{16,0},{1,17},{17,1},{2,18},{18,2},{3,19},{19,3},{4,20},{20... | collective-permute-start | bytes 14155784 | tf_op jit(solution)/shard_map/ppermute | solution.py:202
  419.6 12.1 %collective-permute-start.56 = (bf16[16,112,768]{2,1,0:T(8,128)(2,1)}, bf16[16,112,768]{2,1,0:T(8,128)(2,1)}, u32[]{:S(2)}, u32[]{:S(2)}) collective-permute-start(bf16[16,112,768]{2,1,0:T(8,128)(2,1)} %broadcast_select_fusion.7), channel_id=1, source_target_pairs={{0,16},{16,0},{1,17},{17,1},{2,18},{18,2},{3,19},{19,3},{4,20},{20... | collective-permute-start | bytes 8257544 | tf_op jit(solution)/shard_map/ppermute | solution.py:202
  524.1 116.8 %collective-permute-start.57 = (f32[512,768]{1,0:T(8,128)}, f32[512,768]{1,0:T(8,128)}, u32[]{:S(2)}, u32[]{:S(2)}) collective-permute-start(f32[512,768]{1,0:T(8,128)} %get-tuple-element.48), channel_id=1, source_target_pairs={{0,16},{16,0},{1,17},{17,1},{2,18},{18,2},{3,19},{19,3},{4,20},{20... | collective-permute-start | bytes 4718600 | tf_op jit(solution)/shard_map/ppermute | solution.py:202
  525.0 15.7 %collective-permute-start.79 = (bf16[2,1,2,2,32,768]{5,4,3,2,1,0:T(8,128)(2,1)}, bf16[2,1,2,2,32,768]{5,4,3,2,1,0:T(8,128)(2,1)}, u32[]{:S(2)}, u32[]{:S(2)}) collective-permute-start(bf16[2,1,2,2,32,768]{5,4,3,2,1,0:T(8,128)(2,1)} %constant_dynamic-slice_fusion.27), channel_id=1, source_target_pairs={{0,4},{1,5},{2,6},{3,7},{4,0},{5,1},{6,2},{7,3},{8,12},{9,13},{10,... | collective-permute-start | bytes 1179656 | tf_op jit(solution)/shard_map/ppermute | solution.py:218
  526.4 16.9 %collective-permute-start.75 = (bf16[2,2,1,2,40,768]{5,4,3,2,1,0:T(8,128)(2,1)}, bf16[2,2,1,2,40,768]{5,4,3,2,1,0:T(8,128)(2,1)}, u32[]{:S(2)}, u32[]{:S(2)}) collective-permute-start(bf16[2,2,1,2,40,768]{5,4,3,2,1,0:T(8,128)(2,1)} %constant_dynamic-slice_fusion.31), channel_id=1, source_target_pairs={{0,2},{1,3},{2,0},{3,1},{4,6},{5,7},{6,4},{7,5},{8,10},{9,11},{10,... | collective-permute-start | bytes 1474568 | tf_op jit(solution)/shard_map/ppermute | solution.py:218
  528.1 16.7 %collective-permute-start.71 = (bf16[2,2,2,1,40,768]{5,4,3,2,1,0:T(8,128)(2,1)}, bf16[2,2,2,1,40,768]{5,4,3,2,1,0:T(8,128)(2,1)}, u32[]{:S(2)}, u32[]{:S(2)}) collective-permute-start(bf16[2,2,2,1,40,768]{5,4,3,2,1,0:T(8,128)(2,1)} %constant_dynamic-slice_fusion.35), channel_id=1, source_target_pairs={{0,1},{1,0},{2,3},{3,2},{4,5},{5,4},{6,7},{7,6},{8,9},{9,8},{10,11... | collective-permute-start | bytes 1474568 | tf_op jit(solution)/shard_map/ppermute | solution.py:218
  535.6 99.9 %collective-permute-start.58 = (bf16[16,112,768]{2,1,0:T(8,128)(2,1)}, bf16[16,112,768]{2,1,0:T(8,128)(2,1)}, u32[]{:S(2)}, u32[]{:S(2)}) collective-permute-start(bf16[16,112,768]{2,1,0:T(8,128)(2,1)} %broadcast_select_fusion.6), channel_id=1, source_target_pairs={{0,16},{16,0},{1,17},{17,1},{2,18},{18,2},{3,19},{19,3},{4,20},{20... | collective-permute-start | bytes 8257544 | tf_op jit(solution)/shard_map/ppermute | solution.py:202
  540.7 31.2 %collective-permute-start.105 = (bf16[2,1,2,2,64,768]{5,4,3,2,1,0:T(8,128)(2,1)S(1)}, bf16[2,1,2,2,64,768]{5,4,3,2,1,0:T(8,128)(2,1)S(1)}, u32[]{:S(2)}, u32[]{:S(2)}) collective-permute-start(bf16[2,1,2,2,64,768]{5,4,3,2,1,0:T(8,128)(2,1)S(1)} %constant_dynamic-slice_fusion.3), channel_id=1, source_target_pairs={{0,4},{1,5},{2,6},{3,7},{4,0},{5,1},{6,2},{7,3},{8,12},{9,13},{10,... | collective-permute-start | bytes 2359304 | tf_op jit(solution)/shard_map/ppermute | solution.py:218
  544.9 20.3 %collective-permute-start.76 = (bf16[2,1,1,2,40,768]{5,4,3,2,1,0:T(8,128)(2,1)S(1)}, bf16[2,1,1,2,40,768]{5,4,3,2,1,0:T(8,128)(2,1)S(1)}, u32[]{:S(2)}, u32[]{:S(2)}) collective-permute-start(bf16[2,1,1,2,40,768]{5,4,3,2,1,0:T(8,128)(2,1)S(1)} %constant_dynamic-slice_fusion.30), channel_id=1, source_target_pairs={{0,4},{1,5},{2,6},{3,7},{4,0},{5,1},{6,2},{7,3},{8,12},{9,13},{10,... | collective-permute-start | bytes 737288 | tf_op jit(solution)/shard_map/ppermute | solution.py:218
  554.4 11.9 %collective-permute-start.72 = (bf16[2,2,1,1,40,768]{5,4,3,2,1,0:T(8,128)(2,1)S(1)}, bf16[2,2,1,1,40,768]{5,4,3,2,1,0:T(8,128)(2,1)S(1)}, u32[]{:S(2)}, u32[]{:S(2)}) collective-permute-start(bf16[2,2,1,1,40,768]{5,4,3,2,1,0:T(8,128)(2,1)S(1)} %constant_dynamic-slice_fusion.34), channel_id=1, source_target_pairs={{0,2},{1,3},{2,0},{3,1},{4,6},{5,7},{6,4},{7,5},{8,10},{9,11},{10,... | collective-permute-start | bytes 737288 | tf_op jit(solution)/shard_map/ppermute | solution.py:218
  565.2 18.3 %collective-permute-start.101 = (bf16[2,2,1,2,64,768]{5,4,3,2,1,0:T(8,128)(2,1)S(1)}, bf16[2,2,1,2,64,768]{5,4,3,2,1,0:T(8,128)(2,1)S(1)}, u32[]{:S(2)}, u32[]{:S(2)}) collective-permute-start(bf16[2,2,1,2,64,768]{5,4,3,2,1,0:T(8,128)(2,1)S(1)} %constant_dynamic-slice_fusion.7), channel_id=1, source_target_pairs={{0,2},{1,3},{2,0},{3,1},{4,6},{5,7},{6,4},{7,5},{8,10},{9,11},{10,... | collective-permute-start | bytes 2359304 | tf_op jit(solution)/shard_map/ppermute | solution.py:218
  571.3 18.2 %collective-permute-start.97 = (bf16[2,2,2,1,64,768]{5,4,3,2,1,0:T(8,128)(2,1)S(1)}, bf16[2,2,2,1,64,768]{5,4,3,2,1,0:T(8,128)(2,1)S(1)}, u32[]{:S(2)}, u32[]{:S(2)}) collective-permute-start(bf16[2,2,2,1,64,768]{5,4,3,2,1,0:T(8,128)(2,1)S(1)} %constant_dynamic-slice_fusion.11), channel_id=1, source_target_pairs={{0,1},{1,0},{2,3},{3,2},{4,5},{5,4},{6,7},{7,6},{8,9},{9,8},{10,11... | collective-permute-start | bytes 2359304 | tf_op jit(solution)/shard_map/ppermute | solution.py:218
  571.8 104.1 %collective-permute-start.84 = (bf16[16,192,768]{2,1,0:T(8,128)(2,1)S(1)}, bf16[16,192,768]{2,1,0:T(8,128)(2,1)S(1)}, u32[]{:S(2)}, u32[]{:S(2)}) collective-permute-start(bf16[16,192,768]{2,1,0:T(8,128)(2,1)S(1)} %broadcast_select_fusion), channel_id=1, source_target_pairs={{0,16},{16,0},{1,17},{17,1},{2,18},{18,2},{3,19},{19,3},{4,20},{20... | collective-permute-start | bytes 14155784 | tf_op jit(solution)/shard_map/ppermute | solution.py:202
  591.6 14.4 %collective-permute-start.106 = (bf16[2,1,2,1,64,768]{5,4,3,2,1,0:T(8,128)(2,1)S(1)}, bf16[2,1,2,1,64,768]{5,4,3,2,1,0:T(8,128)(2,1)S(1)}, u32[]{:S(2)}, u32[]{:S(2)}) collective-permute-start(bf16[2,1,2,1,64,768]{5,4,3,2,1,0:T(8,128)(2,1)S(1)} %constant_dynamic-slice_fusion.2), channel_id=1, source_target_pairs={{0,1},{1,0},{2,3},{3,2},{4,5},{5,4},{6,7},{7,6},{8,9},{9,8},{10,11... | collective-permute-start | bytes 1179656 | tf_op jit(solution)/shard_map/ppermute | solution.py:218
  639.7 12.0 %collective-permute-start.63 = (bf16[2,2,1,2,40,768]{5,4,3,2,1,0:T(8,128)(2,1)S(1)}, bf16[2,2,1,2,40,768]{5,4,3,2,1,0:T(8,128)(2,1)S(1)}, u32[]{:S(2)}, u32[]{:S(2)}) collective-permute-start(bf16[2,2,1,2,40,768]{5,4,3,2,1,0:T(8,128)(2,1)S(1)} %constant_dynamic-slice_fusion.43), channel_id=1, source_target_pairs={{0,2},{1,3},{2,0},{3,1},{4,6},{5,7},{6,4},{7,5},{8,10},{9,11},{10,... | collective-permute-start | bytes 1474568 | tf_op jit(solution)/shard_map/ppermute | solution.py:218
  680.0 20.3 %collective-permute-start.93 = (bf16[2,1,2,2,64,768]{5,4,3,2,1,0:T(8,128)(2,1)}, bf16[2,1,2,2,64,768]{5,4,3,2,1,0:T(8,128)(2,1)}, u32[]{:S(2)}, u32[]{:S(2)}) collective-permute-start(bf16[2,1,2,2,64,768]{5,4,3,2,1,0:T(8,128)(2,1)} %constant_dynamic-slice_fusion.15), channel_id=1, source_target_pairs={{0,4},{1,5},{2,6},{3,7},{4,0},{5,1},{6,2},{7,3},{8,12},{9,13},{10,... | collective-permute-start | bytes 2359304 | tf_op jit(solution)/shard_map/ppermute | solution.py:218
  682.2 20.5 %collective-permute-start.89 = (bf16[2,2,1,2,64,768]{5,4,3,2,1,0:T(8,128)(2,1)}, bf16[2,2,1,2,64,768]{5,4,3,2,1,0:T(8,128)(2,1)}, u32[]{:S(2)}, u32[]{:S(2)}) collective-permute-start(bf16[2,2,1,2,64,768]{5,4,3,2,1,0:T(8,128)(2,1)} %constant_dynamic-slice_fusion.19), channel_id=1, source_target_pairs={{0,2},{1,3},{2,0},{3,1},{4,6},{5,7},{6,4},{7,5},{8,10},{9,11},{10,... | collective-permute-start | bytes 2359304 | tf_op jit(solution)/shard_map/ppermute | solution.py:218
  683.4 21.8 %collective-permute-start.85 = (bf16[2,2,2,1,64,768]{5,4,3,2,1,0:T(8,128)(2,1)S(1)}, bf16[2,2,2,1,64,768]{5,4,3,2,1,0:T(8,128)(2,1)S(1)}, u32[]{:S(2)}, u32[]{:S(2)}) collective-permute-start(bf16[2,2,2,1,64,768]{5,4,3,2,1,0:T(8,128)(2,1)S(1)} %constant_dynamic-slice_fusion.23), channel_id=1, source_target_pairs={{0,1},{1,0},{2,3},{3,2},{4,5},{5,4},{6,7},{7,6},{8,9},{9,8},{10,11... | collective-permute-start | bytes 2359304 | tf_op jit(solution)/shard_map/ppermute | solution.py:218
  719.9 11.9 %collective-permute-start.96 = (bf16[1,1,1,1,64,768]{5,4,3,2,1,0:T(8,128)(2,1)S(1)}, bf16[1,1,1,1,64,768]{5,4,3,2,1,0:T(8,128)(2,1)S(1)}, u32[]{:S(2)}, u32[]{:S(2)}) collective-permute-start(bf16[1,1,1,1,64,768]{5,4,3,2,1,0:T(8,128)(2,1)S(1)} %constant_dynamic-slice_fusion.12), channel_id=1, source_target_pairs={{0,8},{1,9},{2,10},{3,11},{4,12},{5,13},{6,14},{7,15},{8,0},{9,1},... | collective-permute-start | bytes 294920 | tf_op jit(solution)/shard_map/ppermute | solution.py:218
  721.0 12.7 %collective-permute-start.92 = (bf16[1,1,1,1,64,768]{5,4,3,2,1,0:T(8,128)(2,1)S(1)}, bf16[1,1,1,1,64,768]{5,4,3,2,1,0:T(8,128)(2,1)S(1)}, u32[]{:S(2)}, u32[]{:S(2)}) collective-permute-start(bf16[1,1,1,1,64,768]{5,4,3,2,1,0:T(8,128)(2,1)S(1)} %constant_dynamic-slice_fusion.16), channel_id=1, source_target_pairs={{0,8},{1,9},{2,10},{3,11},{4,12},{5,13},{6,14},{7,15},{8,0},{9,1},... | collective-permute-start | bytes 294920 | tf_op jit(solution)/shard_map/ppermute | solution.py:218
  (265 other events, 2953.6 us)
